TPU v7x, 128 devices: a whole 4x4x4 slice. The times are simulated.
128 devices in a mesh: lon: 16 (over y_hi, x, core), lat: 8 (over y_lo, z).
Axes of the slice: x: 4, y: 4 (y_hi: 2, y_lo: 2; y = y_hi * 2 + y_lo), z: 4, core: 2. Of those that a mesh axis runs over, the one named last changes fastest.
Arguments:
- tokens: bfloat16 [4, 48, 768, 192], P(None, 'lat', 'lon'), may hold values from -6 to 6
- norm1_gain: float32 [192], replicated, may hold values from 0.1 to 1.9
- w_qkv: bfloat16 [192, 576], replicated, may hold values from -0.4375 to 0.4375
- w_proj: bfloat16 [192, 192], replicated, may hold values from -0.4375 to 0.4375
- bias_table: float32 [2, 8, 6, 3312], P(None, 'lat'), may hold values from -4 to 4
- pos_index: int32 [144, 144], replicated, may hold values from 0 to 3311, as said below
- mask_ids: int32 [48], P('lat'), may hold values from 0 to 7, never falling along the last dimension, each value on 1 to 12 neighbouring positions
- norm2_gain: float32 [192], replicated, may hold values from 0.1 to 1.9
- w_fc1: bfloat16 [192, 768], replicated, may hold values from -0.4375 to 0.4375
- w_fc2: bfloat16 [768, 192], replicated, may hold values from -0.21875 to 0.21875
- cotangent: bfloat16 [4, 48, 768, 192], P(None, 'lat', 'lon'), may hold values from -6 to 6
Outputs:
- block_out: bfloat16 [4, 48, 768, 192], P(None, 'lat', 'lon')
- grad_tokens: bfloat16 [4, 48, 768, 192], P(None, 'lat', 'lon')
- grad_norm1: float32 [192], replicated
- grad_qkv: float32 [192, 576], replicated
- grad_proj: float32 [192, 192], replicated
- grad_table: float32 [2, 8, 6, 3312], P(None, 'lat')
- grad_norm2: float32 [192], replicated
- grad_fc1: float32 [192, 768], replicated
- grad_fc2: float32 [768, 192], replicated
Inputs may be any that keep to these rules, and one draw needn't show every extreme that they name: pos_index[i, j] depends only on the level pair, the row pair and the column offset of tokens i and j of a window, and distinct such triples have distinct entries. mask_ids never falls along latitude; a region holds at most 12 rows.
All inputs are finite; a program needn't handle non-finite values.
Results may differ from a plain program's by a relative error of at most 0.023.
Values may be sent and summed in bfloat16 or wider, within the bound.
A program may use at most 128 MiB of HBM per device.

v0:
```python
import jax
import jax.numpy as jnp
from jax import lax
from jax.sharding import PartitionSpec as P

WZ = 2
WH = 6
WW = 12
POS = 3312


EPS = 1e-05
GELU_K = 0.7978845608
GELU_C = 0.044715


def passed_along(array, axis, by):
    devices = lax.axis_size(axis)
    return lax.ppermute(array, axis, [(i, (i + by) % devices) for i in range(devices)])


def norm_forward(field_in, norm_gain):
    center = field_in - jnp.mean(field_in, axis=-1, keepdims=True)
    inv_std = lax.rsqrt(jnp.mean(center * center, axis=-1, keepdims=True) + EPS)
    normed = center * inv_std
    return (normed, inv_std, (normed * norm_gain).astype(jnp.bfloat16))


def norm_backward(d_output, normed, inv_std, norm_gain):
    d_norm = d_output * norm_gain
    mean_grad = jnp.mean(d_norm, axis=-1, keepdims=True)
    mean_prod = jnp.mean(d_norm * normed, axis=-1, keepdims=True)
    return inv_std * (d_norm - mean_grad - normed * mean_prod)


def mult(form, left, right):
    return jnp.einsum(form, left, right, preferred_element_type=jnp.float32)


def window_split(field_in):
    levels, row_count, col_count, feature = field_in.shape
    win_part = field_in.reshape(levels // WZ, WZ, row_count // WH, WH, col_count // WW, WW, feature)
    win_part = win_part.transpose(0, 2, 4, 1, 3, 5, 6)
    return win_part.reshape(levels // WZ, row_count // WH, col_count // WW, WZ * WH * WW, feature)


def window_join(win_part):
    zone_w, row_w, col_w, win_size, feature = win_part.shape
    full_field = win_part.reshape(zone_w, row_w, col_w, WZ, WH, WW, feature).transpose(
        0, 3, 1, 4, 2, 5, 6
    )
    return full_field.reshape(zone_w * WZ, row_w * WH, col_w * WW, feature)


def window_allowed(mask_ids, levels):
    row_count = mask_ids.shape[0]
    top_flag = (jnp.arange(levels) == levels - 1).astype(jnp.int32)
    zone_ids = top_flag[:, None] + 2 * mask_ids[None, :]
    zone_ids = zone_ids.reshape(levels // WZ, WZ, row_count // WH, WH).transpose(0, 2, 1, 3)
    zone_ids = jnp.broadcast_to(zone_ids[..., None], zone_ids.shape + (WW,))
    zone_ids = zone_ids.reshape(levels // WZ, row_count // WH, WZ * WH * WW)
    return (zone_ids[..., :, None] == zone_ids[..., None, :]).astype(jnp.float32)


def attend_forward(windows, w_qkv, w_proj, bias, allowed):
    groups, win_count, win_size, feature = windows.shape
    head_count = bias.shape[1]
    head_dim = feature // head_count
    score_scale = head_dim ** (-0.5)
    proj_qkv = jnp.dot(
        windows.reshape(-1, feature), w_qkv, preferred_element_type=jnp.float32
    ).astype(jnp.bfloat16)
    proj_qkv = proj_qkv.reshape(groups, win_count, win_size, 3, head_count, head_dim)
    queries = proj_qkv[:, :, :, 0]
    key_rows = proj_qkv[:, :, :, 1]
    values = proj_qkv[:, :, :, 2]
    scores = mult("gbqhd,gbkhd->gbhqk", queries, key_rows) * score_scale + bias[:, None]
    weighted = jnp.exp(scores) * allowed[:, None, None]
    attn_prob = weighted / jnp.sum(weighted, axis=-1, keepdims=True)
    prob_low = attn_prob.astype(jnp.bfloat16)
    attended = (
        mult("gbhqk,gbkhd->gbqhd", prob_low, values).astype(jnp.bfloat16).reshape(-1, feature)
    )
    win_out = jnp.dot(attended, w_proj, preferred_element_type=jnp.float32).astype(jnp.bfloat16)
    return (
        win_out.reshape(windows.shape),
        (queries, key_rows, values, attn_prob, prob_low, attended),
    )


def attend_backward(windows, w_qkv, w_proj, saved, d_output):
    queries, key_rows, values, attn_prob, prob_low, attended = saved
    groups, win_count, win_size, feature = windows.shape
    head_count = queries.shape[-2]
    head_dim = queries.shape[-1]
    score_scale = head_dim ** (-0.5)
    d_flat = d_output.reshape(-1, feature)
    grad_proj = jnp.dot(attended.T, d_flat, preferred_element_type=jnp.float32)
    d_att = jnp.dot(d_flat, w_proj.T, preferred_element_type=jnp.float32).astype(jnp.bfloat16)
    d_att = d_att.reshape(groups, win_count, win_size, head_count, head_dim)
    d_prob = mult("gbqhd,gbkhd->gbhqk", d_att, values)
    d_values = mult("gbhqk,gbqhd->gbkhd", prob_low, d_att).astype(jnp.bfloat16)
    d_scores = attn_prob * (d_prob - jnp.sum(attn_prob * d_prob, axis=-1, keepdims=True))
    d_low = (d_scores * score_scale).astype(jnp.bfloat16)
    d_queries = mult("gbhqk,gbkhd->gbqhd", d_low, key_rows).astype(jnp.bfloat16)
    d_keys = mult("gbhqk,gbqhd->gbkhd", d_low, queries).astype(jnp.bfloat16)
    d_qkv = jnp.stack([d_queries, d_keys, d_values], axis=3).reshape(-1, 3 * feature)
    grad_qkv = jnp.dot(windows.reshape(-1, feature).T, d_qkv, preferred_element_type=jnp.float32)
    d_windows = jnp.dot(d_qkv, w_qkv.T, preferred_element_type=jnp.float32).astype(jnp.bfloat16)
    return (d_windows.reshape(windows.shape), grad_qkv, grad_proj, jnp.sum(d_scores, axis=1))


def table_terms(d_bias, pos_index, entries):
    groups, head_count, win_size, _ = d_bias.shape
    flat_in = d_bias.reshape(groups * head_count, win_size * win_size).T
    summed = jax.ops.segment_sum(flat_in, pos_index.reshape(-1), num_segments=entries)
    return summed.T.reshape(groups, head_count, entries)


def mlp_pass(mid_field, cot_rows, norm_gain, w_fc1, w_fc2):
    normed, inv_std, hidden = norm_forward(mid_field, norm_gain)
    pre_act = jnp.dot(hidden, w_fc1, preferred_element_type=jnp.float32)
    inner = jnp.tanh(GELU_K * (pre_act + GELU_C * pre_act * pre_act * pre_act))
    act_low = (0.5 * pre_act * (1.0 + inner)).astype(jnp.bfloat16)
    block_rows = (mid_field + jnp.dot(act_low, w_fc2, preferred_element_type=jnp.float32)).astype(
        jnp.bfloat16
    )
    grad_fc2 = jnp.dot(act_low.T, cot_rows, preferred_element_type=jnp.float32)
    d_act = jnp.dot(cot_rows, w_fc2.T, preferred_element_type=jnp.float32)
    slope = 0.5 * (1.0 + inner) + 0.5 * pre_act * (1.0 - inner * inner) * GELU_K * (
        1.0 + 3.0 * GELU_C * pre_act * pre_act
    )
    d_pre = (d_act * slope).astype(jnp.bfloat16)
    grad_fc1 = jnp.dot(hidden.T, d_pre, preferred_element_type=jnp.float32)
    d_hidden = jnp.dot(d_pre, w_fc1.T, preferred_element_type=jnp.float32)
    grad_gain = jnp.sum(d_hidden * normed, axis=0)
    d_mid = cot_rows.astype(jnp.float32) + norm_backward(d_hidden, normed, inv_std, norm_gain)
    return (block_rows, d_mid, grad_gain, grad_fc1, grad_fc2)


def roll_ahead(field_in):
    half_rows = WH // 2
    half_cols = WW // 2
    field_in = jnp.roll(field_in, -1, axis=-4)
    got_rows = passed_along(field_in[..., :half_rows, :, :], "lat", -1)
    field_in = jnp.concatenate([field_in[..., half_rows:, :, :], got_rows], axis=-3)
    got_cols = passed_along(field_in[..., :half_cols, :], "lon", -1)
    return jnp.concatenate([field_in[..., half_cols:, :], got_cols], axis=-2)


def roll_behind(field_in):
    row_count = field_in.shape[-3]
    col_count = field_in.shape[-2]
    half_rows = WH // 2
    half_cols = WW // 2
    got_cols = passed_along(field_in[..., col_count - half_cols :, :], "lon", 1)
    field_in = jnp.concatenate([got_cols, field_in[..., : col_count - half_cols, :]], axis=-2)
    got_rows = passed_along(field_in[..., row_count - half_rows :, :, :], "lat", 1)
    moved = jnp.concatenate([got_rows, field_in[..., : row_count - half_rows, :, :]], axis=-3)
    return jnp.roll(moved, 1, axis=-4)


def inner_ahead(field_in):
    return roll_ahead(field_in)


def inner_behind(field_in):
    return roll_behind(field_in)


def to_groups(win_part):
    zone_w, row_w, col_w, win_size, feature = win_part.shape
    return win_part.reshape(zone_w * row_w, col_w, win_size, feature)


def shards(
    tokens,
    norm1_gain,
    w_qkv,
    w_proj,
    bias_table,
    pos_index,
    mask_ids,
    norm2_gain,
    w_fc1,
    w_fc2,
    cotangent,
):
    levels, row_count, col_count, feature = tokens.shape
    field = tokens.astype(jnp.float32)
    normed1, inv_std1, hidden = norm_forward(field, norm1_gain)
    split_in = window_split(inner_ahead(hidden))
    grid_shape = split_in.shape
    windows = to_groups(split_in)
    zone_w, row_w = (bias_table.shape[0], bias_table.shape[1])
    bias = jnp.take(bias_table, pos_index, axis=3)
    bias = bias.reshape(zone_w * row_w, bias.shape[2], bias.shape[3], bias.shape[4])
    allowed = window_allowed(mask_ids, levels)
    allowed = allowed.reshape(zone_w * row_w, allowed.shape[2], allowed.shape[3])
    win_out, saved = attend_forward(windows, w_qkv, w_proj, bias, allowed)
    attn_field = inner_behind(window_join(win_out.reshape(grid_shape)))
    mid_field = field + attn_field.astype(jnp.float32)
    block_rows, d_mid, g_norm2, g_fc1, g_fc2 = mlp_pass(
        mid_field.reshape(-1, feature), cotangent.reshape(-1, feature), norm2_gain, w_fc1, w_fc2
    )
    block_here = block_rows.reshape(tokens.shape)
    d_mid = d_mid.reshape(tokens.shape)
    d_attn = to_groups(window_split(inner_ahead(d_mid.astype(jnp.bfloat16))))
    d_win, g_qkv, g_proj, d_bias = attend_backward(windows, w_qkv, w_proj, saved, d_attn)
    local_table = table_terms(d_bias, pos_index, POS).reshape(bias_table.shape)
    table_sum = lax.psum(local_table.astype(jnp.bfloat16), "lon").astype(jnp.float32)
    d_hidden = inner_behind(window_join(d_win.reshape(grid_shape))).astype(jnp.float32)
    g_norm1 = jnp.sum(d_hidden * normed1, axis=(0, 1, 2))
    grad_here = (d_mid + norm_backward(d_hidden, normed1, inv_std1, norm1_gain)).astype(
        jnp.bfloat16
    )
    grads = (g_norm1, g_qkv, g_proj, g_norm2, g_fc1, g_fc2)
    summed = lax.psum((grads[0], grads[1], grads[2], grads[3], grads[4], grads[5]), ("lon", "lat"))
    total_tokens = levels * row_count * col_count * lax.axis_size("lat") * lax.axis_size("lon")
    factor = float(total_tokens) ** (-0.5)
    return (
        block_here,
        grad_here,
        summed[0] * factor,
        summed[1] * factor,
        summed[2] * factor,
        table_sum * factor,
        summed[3] * factor,
        summed[4] * factor,
        summed[5] * factor,
    )


def solution(mesh):
    in_specs = (
        P(None, "lat", "lon", None),
        P(),
        P(),
        P(),
        P(None, "lat", None, None),
        P(),
        P("lat"),
        P(),
        P(),
        P(),
        P(None, "lat", "lon", None),
    )
    out_specs = (
        P(None, "lat", "lon", None),
        P(None, "lat", "lon", None),
        P(),
        P(),
        P(),
        P(None, "lat", None, None),
        P(),
        P(),
        P(),
    )
    return jax.shard_map(shards, mesh=mesh, in_specs=in_specs, out_specs=out_specs, check_vma=False)
```

profile of v0, /device:TPU:1, one launch (start us, length us, event | category | flops | bytes accessed | tf_op | source)
XLA Modules:
  0.0 679.5 jit_solution(17761707547142276509)
XLA Ops:
  14.6 5.6 collective-permute-start
  20.3 3.5 copy.152
  23.9 59.0 %gather_fusion = f32[20736,2,6]{2,1,0:T(2,128)} fusion(f32[2,6,3312]{1,0,2:T(2,128)} %bitcast.106, s32[21504]{0:T(1024)S(1)} %pad_clamp_fusion), kind=kCustom, calls=%fused_computation | custom fusion | bytes 2073600 | tf_op jit(solution)/shard_map/jit(_take)/gather | solution.py:196
  82.9 28.6 %copy.153 = f32[144,144,2,6]{1,0,2,3:T(8,128)S(1)} copy(f32[144,144,2,6]{3,2,1,0:T(2,128)} %bitcast.103) | data formatting | bytes 1990656 | tf_op jit(solution)/shard_map/jit(_take)/gather | solution.py:196
  117.8 2.8 collective-permute-done.1
  125.8 2.8 convolution_convert_fusion
  128.7 8.8 %reshape.182 = bf16[2,4,144,3,6,32]{2,1,0,5,4,3:T(4,128)(2,1)} reshape(bf16[1152,576]{0,1:T(8,128)(2,1)} %convolution_convert_fusion) | data formatting | bytes 2654208 | tf_op jit(solution)/shard_map/reshape | solution.py:73
  137.4 2.6 fusion.69
  152.5 10.0 %collective-permute-start.2 = (bf16[4,6,6,192]{3,0,2,1:T(4,128)(2,1)S(1)}, bf16[4,6,6,192]{3,0,2,1:T(4,128)(2,1)S(1)}, u32[]{:S(2)}, u32[]{:S(2)}) collective-permute-start(bf16[4,6,6,192]{3,0,2,1:T(4,128)(2,1)S(1)} %slice.123), channel_id=1, source_target_pairs={{0,8},{8,16},{16,24},{24,32},{32,40},{40,48},{48,56},{56,64},{64,7... | collective-permute-start | bytes 165896 | tf_op jit(solution)/shard_map/ppermute | solution.py:19
  162.7 3.7 collective-permute-done.2
  169.3 5.0 collective-permute-done.3
  180.4 2.7 multiply_convert_fusion.1
  195.7 2.9 fusion.77
  198.6 8.4 %collective-permute-start.5 = (bf16[4,6,6,192]{3,2,1,0:T(8,128)(2,1)S(1)}, bf16[4,6,6,192]{3,2,1,0:T(8,128)(2,1)S(1)}, u32[]{:S(2)}, u32[]{:S(2)}) collective-permute-start(bf16[4,6,6,192]{3,2,1,0:T(8,128)(2,1)S(1)} %pad_maximum_fusion.8), channel_id=1, source_target_pairs={{0,120},{8,0},{16,8},{24,16},{32,24},{40,32},{48,40},{56,48},{64,5... | collective-permute-start | bytes 165896 | tf_op jit(solution)/shard_map/ppermute | solution.py:19
  213.5 11.0 %fusion.70 = (f32[2,6,144,144]{2,3,1,0:T(8,128)}, f32[2,4,6,144,144]{3,4,2,1,0:T(8,128)}) fusion(f32[2,4,6,144,144]{3,4,2,1,0:T(8,128)} %copy-done.2, bf16[2,4,144,1,6,32]{2,1,0,5,4,3:T(4,128)(2,1)S(1)} %get-tuple-element.59, bf16[2,4,144,6,32]{2,1,0,4,3:T(4,128)(2,1)S(1)} %reshape.190), kind=kOutput, calls=%fused_computation.134 | convolution fusion | flops 131141520 | bytes 9842688 | tf_op jit(solution)/shard_map/sub | solution.py:103
  224.5 4.3 fusion.30
  233.9 3.4 copy.139
  237.3 4.9 reshape.191
  249.3 6.9 %copy.144 = f32[20736,12]{1,0:T(8,128)} copy(f32[20736,12]{0,1:T(8,128)} %bitcast.109) | data formatting | bytes 1990656 | tf_op jit(solution)/shard_map/transpose | solution.py:115
  256.1 113.1 %scatter_custom_fusion = f32[3312,12]{1,0:T(8,128)S(1)} fusion(s32[20736]{0:T(1024)} %reshape.206, f32[20736,12]{1,0:T(8,128)} %copy.144, f32[]{:T(128)} %constant.16.clone.1), kind=kCustom, calls=%fused_computation.68 | custom fusion | flops 248832 | bytes 159488 | tf_op jit(solution)/shard_map/scatter-add | solution.py:116
  376.5 3.1 collective-permute-done.6
  379.9 127.3 %all-reduce.5.cloned.1.call-done = bf16[2,1,6,3312]{3,2,0,1:T(8,128)(2,1)} async-done(((bf16[2,1,6,3312]{3,2,0,1:T(8,128)(2,1)}), bf16[2,1,6,3312]{3,2,0,1:T(8,128)(2,1)}) %all-reduce.5.cloned.1.call-update) | async-done | bytes 79504 | tf_op jit(solution)/shard_map/psum | solution.py:211
  515.4 68.8 %all-reduce = (f32[192]{0:T(256)S(1)}, f32[192]{0:T(256)S(1)}) all-reduce(f32[192]{0:T(256)S(1)} %get-tuple-element.47, f32[192]{0:T(256)S(1)} %get-tuple-element.45), channel_id=1, replica_groups=mesh['lon'=16,'lat'=8] {'lon','lat'}, use_global_device_ids=true, to_apply=%region_11.12 | all-reduce | flops 384 | bytes 3072 | tf_op jit(solution)/shard_map/psum | solution.py:218
  585.4 81.4 %all-reduce.7.cloned.1.call-done = (f32[192,576]{1,0:T(8,128)}, f32[192,192]{1,0:T(8,128)}, f32[192,768]{1,0:T(8,128)}, f32[768,192]{0,1:T(8,128)}) async-done(((f32[192,576]{1,0:T(8,128)}, f32[192,192]{1,0:T(8,128)}, f32[192,768]{1,0:T(8,128)}, f32[768,192]{0,1:T(8,128)}), (f32[192,576]{1,0:T(8,128)}, f32[192,192]{1,0:T(8,128)}, f32[192,768]{1,0:T(8,128)}, ...) | async-done | bytes 1769488 | tf_op jit(solution)/shard_map/psum | solution.py:218
  (197 shorter events, 93.8 us)
Async XLA Ops:
  7.2 173.2 %copy-start = (bf16[192,768]{1,0:T(8,128)(2,1)S(1)}, bf16[192,768]{1,0:T(8,128)(2,1)}, u32[]{:S(2)}) copy-start(bf16[192,768]{1,0:T(8,128)(2,1)} %param.19) | copy-start | bytes 884740
  7.2 500.0 %all-reduce.5.cloned.1.call-start = ((), (), s32[]{:S(2)}) async-start(), calls=%async_computation | async-start | bytes 212992 | tf_op jit(solution)/shard_map/psum | solution.py:211
  9.0 5.6 copy-start.16
  11.0 9.2 %copy-start.24 = (s32[144,144]{1,0:T(8,128)S(1)}, s32[144,144]{1,0:T(8,128)}, u32[]{:S(2)}) copy-start(s32[144,144]{1,0:T(8,128)} %param.16) | copy-start | bytes 248836
  11.0 9.2 %copy-start.32 = (f32[2,1,6,3312]{3,1,2,0:T(1,128)S(1)}, f32[2,1,6,3312]{3,1,2,0:T(1,128)}, u32[]{:S(2)}) copy-start(f32[2,1,6,3312]{3,1,2,0:T(1,128)} %param.15) | copy-start | bytes 476932
  14.6 101.5 %collective-permute-start = (bf16[4,3,48,192]{3,0,2,1:T(4,128)(2,1)}, bf16[4,3,48,192]{3,0,2,1:T(4,128)(2,1)S(1)}, u32[]{:S(2)}, u32[]{:S(2)}) collective-permute-start(bf16[4,3,48,192]{3,0,2,1:T(4,128)(2,1)} %get-tuple-element.63), channel_id=1, source_target_pairs={{0,7},{1,0},{2,1},{3,2},{4,3},{5,4},{6,5},{7,6},{8,15},{9,8},{10,9... | collective-permute-start | bytes 663560 | tf_op jit(solution)/shard_map/ppermute | solution.py:19
  116.2 4.4 collective-permute-start.1
  148.9 19.5 %copy-start.21 = (bf16[4,6,48,192]{3,2,1,0:T(8,128)(2,1)S(1)}, bf16[4,6,48,192]{3,2,1,0:T(8,128)(2,1)}, u32[]{:S(2)}) copy-start(bf16[4,6,48,192]{3,2,1,0:T(8,128)(2,1)} %param.21) | copy-start | bytes 1327108
  152.5 13.9 %collective-permute-start.2 = (bf16[4,6,6,192]{3,0,2,1:T(4,128)(2,1)S(1)}, bf16[4,6,6,192]{3,0,2,1:T(4,128)(2,1)S(1)}, u32[]{:S(2)}, u32[]{:S(2)}) collective-permute-start(bf16[4,6,6,192]{3,0,2,1:T(4,128)(2,1)S(1)} %slice.123), channel_id=1, source_target_pairs={{0,8},{8,16},{16,24},{24,32},{32,40},{40,48},{48,56},{56,64},{64,7... | collective-permute-start | bytes 165896 | tf_op jit(solution)/shard_map/ppermute | solution.py:19
  166.6 7.8 %collective-permute-start.3 = (bf16[4,3,48,192]{3,0,2,1:T(4,128)(2,1)S(1)}, bf16[4,3,48,192]{3,0,2,1:T(4,128)(2,1)S(1)}, u32[]{:S(2)}, u32[]{:S(2)}) collective-permute-start(bf16[4,3,48,192]{3,0,2,1:T(4,128)(2,1)S(1)} %fusion.62), channel_id=1, source_target_pairs={{0,1},{1,2},{2,3},{3,4},{4,5},{5,6},{6,7},{7,0},{8,9},{9,10},{10,1... | collective-permute-start | bytes 663560 | tf_op jit(solution)/shard_map/ppermute | solution.py:19
  192.1 6.5 collective-permute-start.4
  198.6 9.3 %collective-permute-start.5 = (bf16[4,6,6,192]{3,2,1,0:T(8,128)(2,1)S(1)}, bf16[4,6,6,192]{3,2,1,0:T(8,128)(2,1)S(1)}, u32[]{:S(2)}, u32[]{:S(2)}) collective-permute-start(bf16[4,6,6,192]{3,2,1,0:T(8,128)(2,1)S(1)} %pad_maximum_fusion.8), channel_id=1, source_target_pairs={{0,120},{8,0},{16,8},{24,16},{32,24},{40,32},{48,40},{56,48},{64,5... | collective-permute-start | bytes 165896 | tf_op jit(solution)/shard_map/ppermute | solution.py:19
  213.5 15.3 %copy-start.8 = (bf16[2,4,144,1,6,32]{2,1,0,5,4,3:T(4,128)(2,1)S(1)}, bf16[2,4,144,1,6,32]{2,1,0,5,4,3:T(4,128)(2,1)}, u32[]{:S(2)}) copy-start(bf16[2,4,144,1,6,32]{2,1,0,5,4,3:T(4,128)(2,1)} %copy-done.7) | copy-start | bytes 1327108
  224.5 5.3 copy-start.3
  224.5 6.5 slice-start
  237.3 4.9 copy-start.13
  237.3 6.4 copy-start.25
  372.4 294.4 %all-reduce.7.cloned.1.call-start = ((), (), s32[]{:S(2)}) async-start(), calls=%async_computation.1 | async-start | bytes 3735552 | tf_op jit(solution)/shard_map/psum | solution.py:218
  375.2 4.4 collective-permute-start.6
  376.4 133.3 %copy-start.17 = (f32[4,6,48]{0,2,1:T(8,128)S(1)}, f32[4,6,48]{0,2,1:T(8,128)}, u32[]{:S(2)}) copy-start(f32[4,6,48]{0,2,1:T(8,128)} %copy-done.16) | copy-start | bytes 13828
  376.5 133.3 %copy-start.20 = (f32[4,6,48]{0,2,1:T(8,128)S(1)}, f32[4,6,48]{0,2,1:T(8,128)}, u32[]{:S(2)}) copy-start(f32[4,6,48]{0,2,1:T(8,128)} %copy-done.19) | copy-start | bytes 13828
  376.5 133.3 %copy-start.33 = (f32[192]{0:T(256)S(1)}, f32[192]{0:T(256)}, u32[]{:S(2)}) copy-start(f32[192]{0:T(256)} %param.12) | copy-start | bytes 2308
  379.8 129.2 %collective-permute-start.7 = (bf16[4,3,48,192]{3,0,2,1:T(4,128)(2,1)S(1)}, bf16[4,3,48,192]{3,0,2,1:T(4,128)(2,1)S(1)}, u32[]{:S(2)}, u32[]{:S(2)}) collective-permute-start(bf16[4,3,48,192]{3,0,2,1:T(4,128)(2,1)S(1)} %fusion.60), channel_id=1, source_target_pairs={{0,1},{1,2},{2,3},{3,4},{4,5},{5,6},{6,7},{7,0},{8,9},{9,10},{10,1... | collective-permute-start | bytes 663560 | tf_op jit(solution)/shard_map/ppermute | solution.py:19
  512.2 160.1 %copy-start.1 = (bf16[192,768]{1,0:T(8,128)(2,1)S(1)}, bf16[192,768]{1,0:T(8,128)(2,1)}, u32[]{:S(2)}) copy-start(bf16[192,768]{1,0:T(8,128)(2,1)} %param.19) | copy-start | bytes 884740
  (24 other events, 65.8 us)
Sparse Core Ops, SparseCore 0:
  372.5 134.6 all-reduce.4
  514.2 152.5 all-reduce.6
where the time goes:
time: 689 us; the launch traced here: 680 us
  waiting for transfers between devices  224 us (33%)
  local copies, waits for them, and re-layouts  161 us (23%)
  other arithmetic  144 us (21%)
  blocking collectives  68.8 us (10%)
  matrix products  39.9 us (6%)
  starting transfers between devices  25.6 us (4%)
  between operations  15.3 us (2%)
    psum x1, waiting for transfers between devices, shards(): lax.psum(local_table.astype(jnp.bfloat16), 'lon').astype(jnp.float32)  127 us
    scatter-add x1, other arithmetic, table_terms(): jax.ops.segment_sum(flat_in, pos_index.reshape(-1), num_segments=entries)  113 us
    gather x2, local copies, waits for them, and re-layouts, shards(): bias = jnp.take(bias_table, pos_index, axis=3)  87.5 us
    psum x1, waiting for transfers between devices, shards(): lax.psum((grads[0], grads[1], grads[2], grads[3], grads[4], grads[5]), ('...  81.4 us
    psum x1, blocking collectives, shards(): lax.psum((grads[0], grads[1], grads[2], grads[3], grads[4], grads[5]), ('...  68.8 us
    ppermute x8, starting transfers between devices, passed_along(): lax.ppermute(array, axis, [(i, (i + by) % devices) for i in range(devices)])  25.5 us
    ppermute x8, waiting for transfers between devices, passed_along(): lax.ppermute(array, axis, [(i, (i + by) % devices) for i in range(devices)])  15.3 us
  transfers between devices with their start and end apart: 10, of which 7 were waited for; matrix products, arithmetic and copies ran while one was open for 18% of the time, Pallas kernels for 0%

commit v1 on v0

v1 whole, which is shorter than its diff:
```python
import jax
import jax.numpy as jnp
from jax import lax
from jax.experimental import pallas as pl
from jax.experimental.pallas import tpu as pltpu
from jax.sharding import PartitionSpec as P

F32 = jnp.float32
BF16 = jnp.bfloat16
C = 192
HEADS = 6
FFN = 768
WIN = 144
NWIN = 8
TOK = 1152
POS = 3312
EPS = 1e-05
GELU_K = 0.7978845608
GELU_C = 0.044715
LOG2E = 1.4426950408889634
LN2 = 0.6931471805599453
SCALE = 32 ** -0.5
FACTOR = 147456.0 ** -0.5


def nn(a, b):
    return lax.dot_general(a, b, (((1,), (0,)), ((), ())), preferred_element_type=F32)


def nt(a, b):
    return lax.dot_general(a, b, (((1,), (1,)), ((), ())), preferred_element_type=F32)


def tn(a, b):
    return lax.dot_general(a, b, (((0,), (0,)), ((), ())), preferred_element_type=F32)


def head_mask(h, dtype):
    lane = lax.broadcasted_iota(jnp.int32, (1, C), 1)
    inside = (lane >= h * 32) & (lane < h * 32 + 32)
    return jnp.where(inside, 1.0, 0.0).astype(dtype)


def spread_heads(x):
    return jnp.concatenate([x * head_mask(h, BF16) for h in range(HEADS)], axis=0)


def pick_heads(x):
    total = x[:WIN] * head_mask(0, F32)
    for h in range(1, HEADS):
        total = total + x[h * WIN : (h + 1) * WIN] * head_mask(h, F32)
    return total


def mean_of(x):
    return jnp.sum(x, axis=-1, keepdims=True) * (1.0 / C)


def norm_stats(x):
    center = x - mean_of(x)
    inv = lax.rsqrt(mean_of(center * center) + EPS)
    return center * inv, inv


def norm_back(g, normed, inv):
    return inv * (g - mean_of(g) - normed * mean_of(g * normed))


def prep_bias(table_ref, idx_ref, mask_ref, bias_ref):
    sub = lax.broadcasted_iota(jnp.int32, (16, 256), 0)
    lane = lax.broadcasted_iota(jnp.int32, (16, 256), 1)
    lane_row = lane // 12
    col = lane - lane_row * 12
    top_i = jnp.where(sub >= 6, 1, 0)
    top_j = jnp.where(lane_row >= 6, 1, 0)
    row_i = sub - 6 * top_i
    row_j = lane_row - 6 * top_j
    zone_i = jnp.zeros((16, 256), jnp.int32)
    zone_j = jnp.zeros((16, 256), jnp.int32)
    for r in range(6):
        zone_i = jnp.where(row_i == r, 2 * mask_ref[r], zone_i)
        zone_j = jnp.where(row_j == r, 2 * mask_ref[r], zone_j)
    idx = idx_ref[...]
    hi = idx >> 7
    lo = idx & 127

    def one(zh, carry):
        row = table_ref[zh] * LOG2E
        tiles = []
        for t in range(2):
            lo_t = lo[:, t * 128 : (t + 1) * 128]
            hi_t = hi[:, t * 128 : (t + 1) * 128]
            acc = jnp.zeros((32, 128), F32)
            for a in range(26):
                part = row[:, a * 128 : min(POS, (a + 1) * 128)]
                if a == 25:
                    part = jnp.concatenate([part, jnp.zeros((1, 16), F32)], axis=1)
                got = jnp.take_along_axis(jnp.broadcast_to(part, (32, 128)), lo_t, axis=1)
                acc = jnp.where(hi_t == a, got, acc)
            tiles.append(acc)
        both = jnp.concatenate(tiles, axis=1)
        upper, lower = both[:16], both[16:]
        flag = jnp.where(zh >= HEADS, 1, 0)
        same = (zone_i + top_i * flag) == (zone_j + top_j * flag)
        mask = jnp.where(same, 0.0, -1e30)
        for c in range(12):
            ahead = pltpu.roll(upper, c, 1) if c else upper
            val = jnp.where(col >= c, ahead, pltpu.roll(lower, 256 - 12 + c, 1)) + mask
            bias_ref[0, zh, pl.ds(c, 12, stride=12), :] = val[:12, :128]
            bias_ref[1, zh, pl.ds(c, 12, stride=12), :] = val[:12, 128:]
        return carry

    lax.fori_loop(0, 12, one, 0)


def assemble(ext_ref, win_ref):
    for level in range(4):
        for r in range(6):
            slab = ext_ref[(level + 1) % 4, r, :, :].astype(F32)
            for w in range(4):
                start = ((level // 2) * 4 + w) * WIN + ((level % 2) * 6 + r) * 12
                win_ref[start : start + 12, :] = slab[6 + 12 * w : 18 + 12 * w]


def disassemble(win_ref, slab_ref, ext_ref):
    for level in range(4):
        for r in range(6):
            k = r % 2
            for w in range(4):
                start = ((level // 2) * 4 + w) * WIN + ((level % 2) * 6 + r) * 12
                slab_ref[k, 6 + 12 * w : 18 + 12 * w, :] = win_ref[start : start + 12, :]
            ext_ref[(level + 1) % 4, r, :, :] = slab_ref[k].astype(BF16)


def forward_window(wi, s):
    rows = pl.ds(pl.multiple_of(wi * WIN, WIN), WIN)
    z = wi // 4
    x = s.x[rows, :]
    normed1, inv1 = norm_stats(x)
    hid = (normed1 * s.n1[...]).astype(BF16)
    s.normed1[rows, :] = normed1
    s.inv1[rows, :] = inv1
    s.hid[rows, :] = hid
    q = (nn(hid, s.wq[0]) * (SCALE * LOG2E)).astype(BF16)
    k = nn(hid, s.wq[1]).astype(BF16)
    v = nn(hid, s.wq[2]).astype(BF16)
    s.k[rows, :] = k
    s.v[rows, :] = v
    qm = spread_heads(q)
    s.q[rows, :] = q
    scores = nt(qm, k)
    b0 = s.bias[0, pl.ds(z * 6, 6)].reshape(864, 128)
    b1 = s.bias[1, pl.ds(z * 6, 6)].reshape(864, 128)
    bias = jnp.concatenate([b0, b1], axis=1)[:, :WIN]
    e = jnp.exp2(scores + bias)
    p = (e * (1.0 / jnp.sum(e, axis=-1, keepdims=True))).astype(BF16)
    s.p[wi] = p
    att = pick_heads(nn(p, v)).astype(BF16)
    s.att[rows, :] = att
    mid = x + nn(att, s.wp[...]).astype(BF16).astype(F32)
    normed2, inv2 = norm_stats(mid)
    hid2 = (normed2 * s.n2[...]).astype(BF16)
    s.hid2[rows, :] = hid2
    pre = nn(hid2, s.w1[...])
    u = pre * pre
    t = jnp.tanh(pre * (GELU_K + (GELU_K * GELU_C) * u))
    half = 0.5 + 0.5 * t
    act = pre * half
    slope = half + act * (1.0 - half) * (2.0 * GELU_K + (6.0 * GELU_K * GELU_C) * u)
    act = act.astype(BF16)
    s.act[rows, :] = act
    s.blk[rows, :] = mid + nt(act, s.w2[...])
    cot = s.cot[rows, :]
    d_act = nn(cot.astype(BF16), s.w2[...])
    d_pre = (d_act * slope).astype(BF16)
    s.d_pre[rows, :] = d_pre
    d_hid2 = nt(d_pre, s.w1[...])
    s.gn[1:2, :] += jnp.sum(d_hid2 * normed2, axis=0, keepdims=True)
    s.d_mid[rows, :] = cot + norm_back(d_hid2 * s.n2[...], normed2, inv2)


def backward_window(wi, s):
    rows = pl.ds(pl.multiple_of(wi * WIN, WIN), WIN)
    z = wi // 4
    d_mid = s.d_mid[rows, :]
    d_att = nt(d_mid.astype(BF16), s.wp[...]).astype(BF16)
    dom = spread_heads(d_att)
    v = s.v[rows, :]
    p = s.p[wi]
    d_p = nt(dom, v)
    d_v = tn(p, dom).astype(BF16)
    pf = p.astype(F32)
    pd = pf * d_p
    d_s = pd - pf * jnp.sum(pd, axis=-1, keepdims=True)
    s.d_bias[0, pl.ds(z * 6, 6)] += d_s[:, :128].reshape(6, WIN, 128)
    s.d_bias[1, pl.ds(z * 6, 6), :, 0:16] += d_s[:, 128:].reshape(6, WIN, 16)
    d_low = d_s.astype(BF16)
    d_k = (tn(d_low, spread_heads(s.q[rows, :])) * LN2).astype(BF16)
    d_q = (pick_heads(nn(d_low, s.k[rows, :])) * SCALE).astype(BF16)
    s.dq[rows, :] = d_q
    s.dk[rows, :] = d_k
    s.dv[rows, :] = d_v
    d_win = nt(d_q, s.wq[0]) + nt(d_k, s.wq[1]) + nt(d_v, s.wq[2])
    d_hid = d_win.astype(BF16).astype(F32)
    normed1 = s.normed1[rows, :]
    s.gn[0:1, :] += jnp.sum(d_hid * normed1, axis=0, keepdims=True)
    s.x[rows, :] = d_mid + norm_back(d_hid * s.n1[...], normed1, s.inv1[rows, :])


def table_back(idx_ref, d_bias_ref, can_ref, lhs_ref, out_ref):
    lane = lax.broadcasted_iota(jnp.int32, (12, 256), 1)
    col = lane - (lane // 12) * 12

    def one(zh, carry):
        up = jnp.zeros((12, 256), F32)
        down = jnp.zeros((12, 256), F32)
        for c in range(12):
            x0 = d_bias_ref[0, zh, pl.ds(c, 12, stride=12), :]
            x1 = d_bias_ref[1, zh, pl.ds(c, 12, stride=12), :]
            x = jnp.concatenate([x0, x1], axis=1)
            over = jnp.where(col >= c, x, 0.0)
            up = up + (pltpu.roll(over, 256 - c, 1) if c else over)
            if c:
                down = down + pltpu.roll(x - over, 12 - c, 1)
        can_ref[0, zh, 0:12, :] = up
        can_ref[1, zh, 0:12, :] = down
        return carry

    lax.fori_loop(0, 12, one, 0)
    acc = jnp.zeros((26 * 16, 128), F32)
    entry = lax.broadcasted_iota(jnp.int32, (128, 256), 0)
    for part in range(2):
        for lr in range(12):
            idx = idx_ref[part * 16 + lr : part * 16 + lr + 1, :]
            ok = lax.broadcasted_iota(jnp.int32, (1, 256), 1) < WIN
            if part == 1:
                spot = lax.broadcasted_iota(jnp.int32, (1, 256), 1)
                ok = ok & (spot - (spot // 12) * 12 > 0)
            hi = jnp.where(ok, idx >> 7, 99)
            lo = idx & 127
            here = jnp.where(entry == lo, 1.0, 0.0).astype(BF16)
            d = can_ref[part, :, lr, :]
            for a in range(26):
                lhs_ref[a * 16 : (a + 1) * 16, :] = jnp.where(hi == a, d, 0.0).astype(BF16)
            acc = acc + nt(lhs_ref[...], here)
    out_ref[...] = acc


class Refs:
    pass


NAMES = [
    ("wq", (3, C, C), BF16),
    ("bias", (2, 12, WIN, 128), F32),
    ("d_bias", (2, 12, WIN, 128), F32),
    ("x", (TOK, C), F32),
    ("cot", (TOK, C), F32),
    ("blk", (TOK, C), F32),
    ("d_mid", (TOK, C), F32),
    ("normed1", (TOK, C), F32),
    ("inv1", (TOK, 1), F32),
    ("hid", (TOK, C), BF16),
    ("q", (TOK, C), BF16),
    ("k", (TOK, C), BF16),
    ("v", (TOK, C), BF16),
    ("p", (NWIN, 864, WIN), BF16),
    ("att", (TOK, C), BF16),
    ("hid2", (TOK, C), BF16),
    ("act", (TOK, FFN), BF16),
    ("d_pre", (TOK, FFN), BF16),
    ("dq", (TOK, C), BF16),
    ("dk", (TOK, C), BF16),
    ("dv", (TOK, C), BF16),
    ("gn", (8, C), F32),
    ("gall", (C, FFN), F32),
    ("can", (2, 16, 16, 256), F32),
    ("lhs", (26 * 16, 256), BF16),
    ("tab", (26 * 16, 128), F32),
    ("slab", (2, 64, C), F32),
    ("tab2", (320, 128), F32),
    ("norms", (16, 128), F32),
    ("ext_tok", (4, 6, 64, C), BF16),
    ("ext_cot", (4, 6, 64, C), BF16),
    ("e_blk", (4, 6, 64, C), BF16),
    ("e_tok", (4, 6, 64, C), BF16),
    ("f_own", (2 * C, FFN), BF16),
    ("f_lon", (16, 48, 384), BF16),
    ("f_lat", (8, 48, 384), BF16),
    ("f_fin", (48, 384), BF16),
    ("t_own", (16, 96, 128), BF16),
    ("t_lon", (16, 96, 128), BF16),
    ("t_lat", (8, 96, 128), BF16),
    ("t_fin", (96, 128), BF16),
]


def pack_table(s):
    t_out = s.t_own
    for a in range(26):
        s.tab2[a * 12 : (a + 1) * 12, :] = s.tab[a * 16 : a * 16 + 12, :]
    for p in range(12, 16):
        t_out[p, 0:80, :] = s.tab2[(p - 12) * 80 : (p - 11) * 80, :].astype(BF16)
        t_out[p, 80:96, :] = jnp.zeros((16, 128), BF16)
    t_out[12, 80:96, :] = s.norms[...].astype(BF16)


SEMS = [
    ("local", 10),
    ("in_send", 6),
    ("in_recv", 6),
    ("out_send", 6),
    ("out_recv", 6),
    ("fa_send", 16),
    ("fa_recv", 16),
    ("fb_send", 8),
    ("fb_recv", 8),
    ("fc_send", 16),
    ("fc_recv", 16),
    ("ta_send", 16),
    ("ta_recv", 16),
    ("tb_send", 8),
    ("tb_recv", 8),
    ("tc_send", 16),
    ("tc_recv", 16),
]


def remote(src, dst, send, recv, where):
    return pltpu.make_async_remote_copy(
        src_ref=src, dst_ref=dst, send_sem=send, recv_sem=recv, device_id=where, device_id_type=pl.DeviceIdType.MESH
    )


def each_peer(count, me, start, stop, body):
    def one(p, carry):
        @pl.when(p != me)
        def _():
            body(p)

        return carry

    lax.fori_loop(start, stop, one, 0)


def main_kernel(
    tok, cot, n1, wqkv, wp, table, idx, mask, n2, w1, w2,
    blk_main, blk_cols, gtok_main, gtok_cols, f_res, t_res, *scratch
):
    s = Refs()
    for (name, _, _), ref in zip(NAMES, scratch):
        setattr(s, name, ref)
    for (name, _), ref in zip(SEMS, scratch[len(NAMES) :]):
        setattr(s, name, ref)
    s.n1, s.n2, s.wp, s.w1, s.w2 = n1, n2, wp, w1, w2
    lon = lax.axis_index("lon")
    lat = lax.axis_index("lat")
    lon_up, lon_down = lax.rem(lon + 1, 16), lax.rem(lon + 15, 16)
    lat_up, lat_down = lax.rem(lat + 1, 8), lax.rem(lat + 7, 8)
    barrier = pltpu.get_barrier_semaphore()

    def greet(a, b):
        pl.semaphore_signal(
            barrier, inc=1, device_id={"lon": a, "lat": b}, device_id_type=pl.DeviceIdType.MESH
        )

    each_peer(16, lon, 0, 16, lambda p: greet(p, lat))
    each_peer(8, lat, 0, 8, lambda p: greet(lon, p))
    greet(lon_up, lat_up)
    greet(lon_down, lat_down)

    locals_in = []
    for i, (src, dst) in enumerate(((tok, s.ext_tok), (cot, s.ext_cot))):
        copy = pltpu.make_async_copy(src.at[:, 3:6], dst.at[:, 0:3, 0:48], s.local.at[i])
        copy.start()
        locals_in.append(copy)
    pl.semaphore_wait(barrier, 24)
    halo_in = []
    for i, (src, dst) in enumerate(((tok, s.ext_tok), (cot, s.ext_cot))):
        moves = (
            (src.at[:, 0:3], dst.at[:, 3:6, 0:48], {"lon": lon, "lat": lat_down}),
            (src.at[:, 3:6, 0:16], dst.at[:, 0:3, 48:64], {"lon": lon_down, "lat": lat}),
            (src.at[:, 0:3, 0:16], dst.at[:, 3:6, 48:64], {"lon": lon_down, "lat": lat_down}),
        )
        for k, (a, b, where) in enumerate(moves):
            copy = remote(a, b, s.in_send.at[3 * i + k], s.in_recv.at[3 * i + k], where)
            copy.start()
            halo_in.append(copy)

    for i in range(3):
        s.wq[i] = wqkv[:, i * C : (i + 1) * C]
    for ref in (s.d_bias, s.gn, s.can, s.slab, s.tab2, s.norms):
        ref[...] = jnp.zeros_like(ref)
    prep_bias(table, idx, mask, s.bias)
    locals_in[0].wait()
    for copy in halo_in[:3]:
        copy.wait_recv()
    assemble(s.ext_tok, s.x)
    locals_in[1].wait()
    for copy in halo_in[3:]:
        copy.wait_recv()
    assemble(s.ext_cot, s.cot)
    for copy in halo_in:
        copy.wait_send()

    def window_loop(body, start, stop):
        lax.fori_loop(start, stop, lambda i, c: (body(i, s), c)[1], 0)

    def send_out(i, e, main, cols):
        copy = pltpu.make_async_copy(e.at[:, 0:3, 0:48], main.at[:, 3:6], s.local.at[2 + i])
        copy.start()
        copies = [copy]
        moves = (
            (e.at[:, 3:6, 0:48], main.at[:, 0:3], {"lon": lon, "lat": lat_up}),
            (e.at[:, 0:3, 48:64], cols.at[:, 3:6], {"lon": lon_up, "lat": lat}),
            (e.at[:, 3:6, 48:64], cols.at[:, 0:3], {"lon": lon_up, "lat": lat_up}),
        )
        for k, (a, b, where) in enumerate(moves):
            copy = remote(a, b, s.out_send.at[3 * i + k], s.out_recv.at[3 * i + k], where)
            copy.start()
            copies.append(copy)
        return copies

    def lon_scatter(piece, slots, send, recv, start, stop):
        def go(p):
            remote(piece(p), slots.at[lon], send.at[p], recv.at[lon], {"lon": p, "lat": lat}).start()

        each_peer(16, lon, start, stop, go)

    def lon_scatter_wait(piece, slots, send, recv):
        def done(p):
            copy = remote(piece(p), slots.at[p], send.at[p], recv.at[p], {"lon": p, "lat": lat})
            copy.wait_send()
            copy.wait_recv()

        each_peer(16, lon, 0, 16, done)

    def lat_spread(slots, send, recv):
        def go(p):
            remote(slots.at[lat], slots.at[lat], send.at[p], recv.at[lat], {"lon": lon, "lat": p}).start()

        each_peer(8, lat, 0, 8, go)

    def lat_spread_wait(slots, send, recv):
        def done(p):
            copy = remote(slots.at[lat], slots.at[p], send.at[p], recv.at[p], {"lon": lon, "lat": p})
            copy.wait_send()
            copy.wait_recv()

        each_peer(8, lat, 0, 8, done)

    def lon_spread(src, slots, local, send, recv):
        pltpu.make_async_copy(src, slots.at[lon], local).start()

        def go(p):
            remote(src, slots.at[lon], send.at[p], recv.at[lon], {"lon": p, "lat": lat}).start()

        each_peer(16, lon, 0, 16, go)

    def lon_spread_wait(src, slots, local, send, recv):
        pltpu.make_async_copy(src, slots.at[lon], local).wait()

        def done(p):
            copy = remote(src, slots.at[p], send.at[p], recv.at[p], {"lon": p, "lat": lat})
            copy.wait_send()
            copy.wait_recv()

        each_peer(16, lon, 0, 16, done)

    def f_piece(p):
        g = p // 2
        half = p - 2 * g
        return s.f_own.at[pl.ds(pl.multiple_of(g * 48, 48), 48), pl.ds(pl.multiple_of(half * 384, 384), 384)]

    def t_piece(p):
        return s.t_own.at[p]

    def total(slots, count):
        acc = slots[0].astype(F32)
        for i in range(1, count):
            acc = acc + slots[i].astype(F32)
        return acc

    window_loop(forward_window, 0, NWIN)
    s.f_own[0:C, :] = tn(s.hid2[...], s.d_pre[...]).astype(BF16)
    s.f_own[C : 2 * C, :] = tn(s.cot[...].astype(BF16), s.act[...]).astype(BF16)
    lon_scatter(f_piece, s.f_lon, s.fa_send, s.fa_recv, 0, 16)
    s.f_lon[lon] = f_piece(lon)[...]
    disassemble(s.blk, s.slab, s.e_blk)
    out_copies = send_out(0, s.e_blk, blk_main, blk_cols)

    window_loop(backward_window, 0, 3)
    lon_scatter_wait(f_piece, s.f_lon, s.fa_send, s.fa_recv)
    s.f_lat[lat] = total(s.f_lon, 16).astype(BF16)
    lat_spread(s.f_lat, s.fb_send, s.fb_recv)
    window_loop(backward_window, 3, 5)
    lat_spread_wait(s.f_lat, s.fb_send, s.fb_recv)
    s.f_fin[...] = total(s.f_lat, 8).astype(BF16)
    lon_spread(s.f_fin, f_res, s.local.at[4], s.fc_send, s.fc_recv)
    window_loop(backward_window, 5, NWIN)

    hid = s.hid[...]
    s.gall[:, 0:C] = tn(hid, s.dq[...])
    s.gall[:, C : 2 * C] = tn(hid, s.dk[...])
    s.gall[:, 2 * C : 3 * C] = tn(hid, s.dv[...])
    s.gall[:, 3 * C : 4 * C] = tn(s.att[...], s.d_mid[...].astype(BF16))
    for p in range(12):
        for t in range(6):
            part = s.gall[p * 16 : (p + 1) * 16, t * 128 : (t + 1) * 128]
            s.t_own[p, t * 16 : (t + 1) * 16, :] = part.astype(BF16)
    lon_scatter(t_piece, s.t_lon, s.ta_send, s.ta_recv, 0, 12)
    disassemble(s.x, s.slab, s.e_tok)
    out_copies += send_out(1, s.e_tok, gtok_main, gtok_cols)
    table_back(idx, s.d_bias, s.can, s.lhs, s.tab)
    for i in range(2):
        s.norms[2 * i : 2 * i + 1, :] = s.gn[i : i + 1, 0:128]
        s.norms[2 * i + 1 : 2 * i + 2, 0:64] = s.gn[i : i + 1, 128:C]
    pack_table(s)
    lon_scatter(t_piece, s.t_lon, s.ta_send, s.ta_recv, 12, 16)
    s.t_lon[lon] = s.t_own[lon]
    lon_scatter_wait(t_piece, s.t_lon, s.ta_send, s.ta_recv)
    s.t_lat[lat] = total(s.t_lon, 16).astype(BF16)
    lat_spread(s.t_lat, s.tb_send, s.tb_recv)
    lat_spread_wait(s.t_lat, s.tb_send, s.tb_recv)
    sub = lax.broadcasted_iota(jnp.int32, (96, 128), 0)
    keep = (sub < 80) & (jnp.zeros((96, 128), jnp.int32) + lon >= 12)
    s.t_fin[...] = jnp.where(keep, s.t_lat[lat].astype(F32), total(s.t_lat, 8)).astype(BF16)
    lon_spread(s.t_fin, t_res, s.local.at[5], s.tc_send, s.tc_recv)
    lon_spread_wait(s.f_fin, f_res, s.local.at[4], s.fc_send, s.fc_recv)
    out_copies[0].wait()
    out_copies[4].wait()
    for copy in out_copies[1:4] + out_copies[5:]:
        copy.wait_send()
        copy.wait_recv()
    lon_spread_wait(s.t_fin, t_res, s.local.at[5], s.tc_send, s.tc_recv)


def finish_kernel(
    blk_main, blk_cols, gtok_main, gtok_cols, f_res, t_res,
    block, gtok, gn1, gqkv, gproj, gtable, gn2, gfc1, gfc2, w_full, tab2
):
    col = lax.broadcasted_iota(jnp.int32, (16, C), 0)
    for main, cols, out in ((blk_main, blk_cols, block), (gtok_main, gtok_cols, gtok)):
        for level in range(4):
            for r in range(6):
                edge = jnp.where(col < 6, cols[level, r].astype(F32), main[level, r, 0:16, :].astype(F32))
                out[level, r, 0:16, :] = edge.astype(BF16)
                out[level, r, 16:48, :] = main[level, r, 16:48, :]
    for p in range(16):
        out = gfc1 if p < 8 else gfc2
        g, half = (p // 2) % 4, p % 2
        out[g * 48 : (g + 1) * 48, half * 384 : (half + 1) * 384] = f_res[p].astype(F32) * FACTOR
    for p in range(12):
        for t in range(6):
            part = t_res[p, t * 16 : (t + 1) * 16, :].astype(F32) * FACTOR
            w_full[p * 16 : (p + 1) * 16, t * 128 : (t + 1) * 128] = part
    gqkv[...] = w_full[:, 0:576]
    gproj[...] = w_full[:, 576:768]
    for p in range(12, 16):
        tab2[(p - 12) * 80 : (p - 11) * 80, :] = t_res[p, 0:80, :].astype(F32) * FACTOR
    for a in range(26):
        width = min(128, POS - a * 128)
        for k in range(12):
            gtable[k, :, a * 128 : a * 128 + width] = tab2[a * 12 + k : a * 12 + k + 1, 0:width]
    norms = t_res[12, 80:96, :].astype(F32) * FACTOR
    for i, out in enumerate((gn1, gn2)):
        out[:, 0:128] = norms[2 * i : 2 * i + 1, :]
        out[:, 128:C] = norms[2 * i + 1 : 2 * i + 2, 0:64]


def index_tables(pos_index):
    up = pos_index[::12, :]
    down = pos_index[:, ::12].reshape(12, 12, 12)
    down = jnp.concatenate([down[:, :1], down[:, :0:-1]], axis=1).transpose(0, 2, 1).reshape(12, WIN)
    both = jnp.stack([up, down])
    return jnp.pad(both, ((0, 0), (0, 4), (0, 112))).reshape(32, 256)


def shards(tokens, norm1_gain, w_qkv, w_proj, bias_table, pos_index, mask_ids, norm2_gain, w_fc1, w_fc2, cotangent):
    vm = pl.BlockSpec(memory_space=pltpu.VMEM)
    anywhere = pl.BlockSpec(memory_space=pl.ANY)
    main = jax.ShapeDtypeStruct((4, 6, 48, C), BF16)
    cols = jax.ShapeDtypeStruct((4, 6, 16, C), BF16)
    outs = pl.pallas_call(
        main_kernel,
        out_shape=[
            main, cols, main, cols,
            jax.ShapeDtypeStruct((16, 48, 384), BF16),
            jax.ShapeDtypeStruct((16, 96, 128), BF16),
        ],
        in_specs=[anywhere] * 2 + [vm] * 5 + [pl.BlockSpec(memory_space=pltpu.SMEM)] + [vm] * 3,
        out_specs=[anywhere] * 6,
        scratch_shapes=[pltpu.VMEM(shape, dtype) for _, shape, dtype in NAMES]
        + [pltpu.SemaphoreType.DMA((n,)) for _, n in SEMS],
        compiler_params=pltpu.CompilerParams(
            vmem_limit_bytes=56 * 1024 * 1024, collective_id=0, has_side_effects=True
        ),
    )(
        tokens, cotangent, norm1_gain.reshape(1, C), w_qkv, w_proj,
        bias_table.transpose(0, 2, 1, 3).reshape(12, 1, POS), index_tables(pos_index), mask_ids,
        norm2_gain.reshape(1, C), w_fc1, w_fc2.T,
    )
    f32 = lambda *shape: jax.ShapeDtypeStruct(shape, F32)
    block, gtok, gn1, gqkv, gproj, gtable, gn2, gfc1, gfc2 = pl.pallas_call(
        finish_kernel,
        out_shape=[main, main, f32(1, C), f32(C, 576), f32(C, C), f32(12, 1, POS), f32(1, C), f32(C, FFN), f32(C, FFN)],
        in_specs=[vm] * 6,
        out_specs=[vm] * 9,
        scratch_shapes=[pltpu.VMEM((C, FFN), F32), pltpu.VMEM((320, 128), F32)],
        compiler_params=pltpu.CompilerParams(vmem_limit_bytes=40 * 1024 * 1024),
    )(*outs)
    gtable = gtable.reshape(2, 6, 1, POS).transpose(0, 2, 1, 3)
    return (block, gtok, gn1.reshape(C), gqkv, gproj, gtable, gn2.reshape(C), gfc1, gfc2.T)


def solution(mesh):
    act = P(None, "lat", "lon", None)
    table = P(None, "lat", None, None)
    return jax.shard_map(
        shards,
        mesh=mesh,
        in_specs=(act, P(), P(), P(), table, P(), P("lat"), P(), P(), P(), act),
        out_specs=(act, act, P(), P(), P(), table, P(), P(), P()),
        check_vma=False,
    )
```

time: 689 us -> 113 us (0.16); the launches traced: 680 us -> 113 us
  waiting for transfers between devices: 224 us -> 0 us
  local copies, waits for them, and re-layouts: 161 us -> 9.24 us
  other arithmetic: 144 us -> 0.1 us
  Pallas kernels: 0 us -> 102 us
  blocking collectives: 68.8 us -> 0 us
  matrix products: 39.9 us -> 0 us
  starting transfers between devices: 25.6 us -> 0 us
  between operations: 15.3 us -> 0.72 us
    psum x2 -> x0, waiting for transfers between devices: 209 us -> none  [the longest x1 127 us: shards(): lax.psum(local_table.astype(jnp.bfloat16), 'lon').astype(jnp.float32)]
    scatter-add x1 -> x0, other arithmetic: 113 us -> none  [table_terms(): jax.ops.segment_sum(flat_in, pos_index.reshape(-1), num_segments=entries)]
    pallas_call x0 -> x2, Pallas kernels: none -> 102 us  [the longest x1 101 us: shards(): pl.pallas_call(main_kernel, out_shape=[main, cols, main, cols, jax.ShapeD...]
    gather x2 -> x0, local copies, waits for them, and re-layouts: 87.5 us -> none  [shards(): bias = jnp.take(bias_table, pos_index, axis=3)]
    psum x1 -> x0, blocking collectives: 68.8 us -> none  [shards(): lax.psum((grads[0], grads[1], grads[2], grads[3], grads[4], grads[5]), ('...]
    dot_general x17 -> x0, matrix products: 28.9 us -> none  [the longest x5 9.74 us: mult(): return jnp.einsum(form, left, right, preferred_element_type=jnp.float32)]
    ppermute x8 -> x0, starting transfers between devices: 25.5 us -> none  [passed_along(): lax.ppermute(array, axis, [(i, (i + by) % devices) for i in range(devices)])]
    reshape x11 -> x1, local copies, waits for them, and re-layouts: 25.3 us -> 0.1 us  [index_tables(): down = pos_index[:, ::12].reshape(12, 12, 12)]
  transfers between devices with their start and end apart: 10 -> 0, of which waited for: 7 -> 0; matrix products, arithmetic and copies ran while one was open for 18% -> 0% of each run, Pallas kernels for 0% -> 0%
where the time goes in v1:
time: 113 us
  Pallas kernels  102 us (90%)
  local copies, waits for them, and re-layouts  9.24 us (8%)
    pallas_call x1, Pallas kernels, shards(): pl.pallas_call(main_kernel, out_shape=[main, cols, main, cols, jax.ShapeD...  101 us
    unnamed x12, local copies, waits for them, and re-layouts  6.03 us

profile of v1, /device:TPU:1, one launch (start us, length us, event | category | flops | bytes accessed | tf_op | source)
XLA Modules:
  0.0 112.6 jit_solution(16204252979509429664)
XLA Ops:
  0.6 0.9 slice.12
  1.6 1.2 %slice.13 = s32[144,12]{1,0:T(8,128)S(1)} slice(s32[144,144]{1,0:T(8,128)} %param.16), slice={[0:144:1], [0:144:12]} | slice | bytes 13824 | tf_op jit(solution)/shard_map/slice | solution.py:573
  2.8 0.1 copy.21
  2.8 0.1 reshape.37
  3.0 0.1 slice.17
  3.0 0.1 rev.3
  3.1 0.1 add_bitcast_fusion
  3.3 0.1 stack_reshape.3
  3.4 0.6 pad.4
  4.0 100.7 %shard_map.178 = (bf16[4,6,48,192]{3,2,1,0:T(8,128)(2,1)}, bf16[4,6,16,192]{3,2,1,0:T(8,128)(2,1)}, bf16[4,6,48,192]{3,2,1,0:T(8,128)(2,1)}, bf16[4,6,16,192]{3,...) custom-call(bf16[4,6,48,192]{3,2,1,0:T(8,128)(2,1)} %tok.1, bf16[4,6,48,192]{3,2,1,0:T(8,128)(2,1)} %cot.1, ...), custom_call_target="tpu_custom_call" | custom-call | tf_op jit(solution)/shard_map/pallas_call | solution.py:584
  104.7 0.0 copy-start
  104.7 1.1 copy-done
  105.8 0.0 copy-start.1
  105.8 1.1 copy-done.1
  106.9 0.0 copy-start.2
  106.9 1.1 copy-done.2
  107.9 0.0 copy-start.3
  107.9 1.0 copy-done.3
  108.9 0.0 copy-start.4
  108.9 0.9 copy-done.4
  109.9 0.0 copy-start.5
  109.9 0.9 copy-done.5
  110.8 1.8 %shard_map.179 = (bf16[4,6,48,192]{3,2,1,0:T(8,128)(2,1)}, bf16[4,6,48,192]{3,2,1,0:T(8,128)(2,1)}, f32[1,192]{1,0:T(1,128)}, f32[192,576]{1,0:T(8,128)}, f32[19...) custom-call(bf16[4,6,48,192]{3,2,1,0:T(8,128)(2,1)S(1)} %copy-done, ...), custom_call_target="tpu_custom_call" | custom-call | tf_op jit(solution)/shard_map/pallas_call | solution.py:604
  (2 shorter events, 0.0 us)
Async XLA Ops:
  104.7 1.1 copy-start
  105.8 1.1 copy-start.1
  106.9 1.1 copy-start.2
  107.9 1.0 copy-start.3
  108.9 0.9 copy-start.4
  109.9 0.9 copy-start.5

commit v2 on v1

v2 whole, which is shorter than its diff:
```python
import jax
import jax.numpy as jnp
from jax import lax
from jax.experimental import pallas as pl
from jax.experimental.pallas import tpu as pltpu
from jax.sharding import PartitionSpec as P

F32 = jnp.float32
BF16 = jnp.bfloat16
C = 192
HEADS = 6
FFN = 768
WIN = 144
NWIN = 8
TOK = 1152
POS = 3312
EPS = 1e-05
GELU_K = 0.7978845608
GELU_C = 0.044715
LOG2E = 1.4426950408889634
LN2 = 0.6931471805599453
SCALE = 32 ** -0.5
FACTOR = 147456.0 ** -0.5


def nn(a, b):
    return lax.dot_general(a, b, (((1,), (0,)), ((), ())), preferred_element_type=F32)


def nt(a, b):
    return lax.dot_general(a, b, (((1,), (1,)), ((), ())), preferred_element_type=F32)


def tn(a, b):
    return lax.dot_general(a, b, (((0,), (0,)), ((), ())), preferred_element_type=F32)


def head_mask(h, dtype):
    lane = lax.broadcasted_iota(jnp.int32, (1, C), 1)
    inside = (lane >= h * 32) & (lane < h * 32 + 32)
    return jnp.where(inside, 1.0, 0.0).astype(dtype)


def spread_heads(x):
    return jnp.concatenate([x * head_mask(h, BF16) for h in range(HEADS)], axis=0)


def pick_heads(x):
    total = x[:WIN] * head_mask(0, F32)
    for h in range(1, HEADS):
        total = total + x[h * WIN : (h + 1) * WIN] * head_mask(h, F32)
    return total


def mean_of(x):
    return jnp.sum(x, axis=-1, keepdims=True) * (1.0 / C)


def norm_stats(x):
    center = x - mean_of(x)
    inv = lax.rsqrt(mean_of(center * center) + EPS)
    return center * inv, inv


def norm_back(g, normed, inv):
    return inv * (g - mean_of(g) - normed * mean_of(g * normed))


def zone_row(mask_ref, out_ref):
    lane = lax.broadcasted_iota(jnp.int32, (8, 128), 1)
    ids = jnp.zeros((8, 128), jnp.int32)
    for r in range(6):
        ids = jnp.where(lane == r, 2 * mask_ref[r], ids)
    out_ref[...] = ids.astype(F32)


def prep_bias(z, table_ref, idx_ref, zone_ref, bias_ref):
    sub = lax.broadcasted_iota(jnp.int32, (16, 256), 0)
    lane = lax.broadcasted_iota(jnp.int32, (16, 256), 1)
    lane_row = lane // 12
    col = lane - lane_row * 12
    top_i = jnp.where(sub >= 6, 1, 0)
    top_j = jnp.where(lane_row >= 6, 1, 0)
    row_i = sub - 6 * top_i
    row_j = lane_row - 6 * top_j
    zone_i = top_i.astype(F32) if z == 1 else jnp.zeros((16, 256), F32)
    zone_j = top_j.astype(F32) if z == 1 else jnp.zeros((16, 256), F32)
    for r in range(6):
        here = jnp.broadcast_to(zone_ref[0:1, r : r + 1], (16, 256))
        zone_i = zone_i + jnp.where(row_i == r, here, 0.0)
        zone_j = zone_j + jnp.where(row_j == r, here, 0.0)
    mask = jnp.where(zone_i == zone_j, 0.0, -1e30)
    idx = idx_ref[...]
    hi = idx >> 7
    lo = idx & 127

    def one(h, carry):
        row = table_ref[h] * LOG2E
        tiles = []
        for t in range(2):
            lo_t = lo[:, t * 128 : (t + 1) * 128]
            hi_t = hi[:, t * 128 : (t + 1) * 128]
            acc = jnp.zeros((32, 128), F32)
            for a in range(26):
                part = row[:, a * 128 : min(POS, (a + 1) * 128)]
                if a == 25:
                    part = jnp.concatenate([part, jnp.zeros((1, 16), F32)], axis=1)
                got = jnp.take_along_axis(jnp.broadcast_to(part, (32, 128)), lo_t, axis=1)
                acc = jnp.where(hi_t == a, got, acc)
            tiles.append(acc)
        both = jnp.concatenate(tiles, axis=1)
        upper, lower = both[:16], both[16:]
        for c in range(12):
            ahead = pltpu.roll(upper, c, 1) if c else upper
            val = jnp.where(col >= c, ahead, pltpu.roll(lower, 256 - 12 + c, 1)) + mask
            bias_ref[0, 6 * z + h, pl.ds(c, 12, stride=12), :] = val[:12, :128]
            bias_ref[1, 6 * z + h, pl.ds(c, 12, stride=12), :] = val[:12, 128:]
        return carry

    lax.fori_loop(0, 6, one, 0)


def assemble(ext_ref, win_ref, z):
    for level in (2 * z, 2 * z + 1):
        for r in range(6):
            slab = ext_ref[(level + 1) % 4, r, :, :].astype(F32)
            for w in range(4):
                start = (z * 4 + w) * WIN + ((level % 2) * 6 + r) * 12
                win_ref[start : start + 12, :] = slab[6 + 12 * w : 18 + 12 * w]


def index_rows(pos_ref, idx_ref):
    idx_ref[...] = jnp.zeros_like(idx_ref)
    for lr in range(12):
        idx_ref[lr : lr + 1, 0:WIN] = pos_ref[lr * 12 : lr * 12 + 1, :]
        idx_ref[16 + lr : 17 + lr, 0:WIN] = pos_ref[lr * 12 + 11 : lr * 12 + 12, :]
    idx_ref[16:32, :] = pltpu.roll(idx_ref[16:32, :], 1, 1)


def disassemble(win_ref, slab_ref, ext_ref):
    for level in range(4):
        for r in range(6):
            k = r % 2
            for w in range(4):
                start = ((level // 2) * 4 + w) * WIN + ((level % 2) * 6 + r) * 12
                slab_ref[k, 6 + 12 * w : 18 + 12 * w, :] = win_ref[start : start + 12, :]
            ext_ref[(level + 1) % 4, r, :, :] = slab_ref[k].astype(BF16)


def attention_window(wi, s):
    rows = pl.ds(pl.multiple_of(wi * WIN, WIN), WIN)
    z = wi // 4
    x = s.x[rows, :]
    normed1, inv1 = norm_stats(x)
    hid = (normed1 * s.n1[...]).astype(BF16)
    s.normed1[rows, :] = normed1
    s.inv1[rows, :] = inv1
    s.hid[rows, :] = hid
    q = (nn(hid, s.wq[0]) * (SCALE * LOG2E)).astype(BF16)
    k = nn(hid, s.wq[1]).astype(BF16)
    v = nn(hid, s.wq[2]).astype(BF16)
    s.k[rows, :] = k
    s.v[rows, :] = v
    qm = spread_heads(q)
    s.q[rows, :] = q
    scores = nt(qm, k)
    b0 = s.bias[0, pl.ds(z * 6, 6)].reshape(864, 128)
    b1 = s.bias[1, pl.ds(z * 6, 6)].reshape(864, 128)
    bias = jnp.concatenate([b0, b1], axis=1)[:, :WIN]
    e = jnp.exp2(scores + bias)
    p = (e * (1.0 / jnp.sum(e, axis=-1, keepdims=True))).astype(BF16)
    s.p[wi] = p
    att = pick_heads(nn(p, v)).astype(BF16)
    s.att[rows, :] = att
    s.blk[rows, :] = x + nn(att, s.wp[...]).astype(BF16).astype(F32)


def mlp_window(wi, s):
    rows = pl.ds(pl.multiple_of(wi * WIN, WIN), WIN)
    mid = s.blk[rows, :]
    normed2, inv2 = norm_stats(mid)
    hid2 = (normed2 * s.n2[...]).astype(BF16)
    s.hid2[rows, :] = hid2
    pre = nn(hid2, s.w1[...])
    u = pre * pre
    t = jnp.tanh(pre * (GELU_K + (GELU_K * GELU_C) * u))
    half = 0.5 + 0.5 * t
    act = pre * half
    slope = half + act * (1.0 - half) * (2.0 * GELU_K + (6.0 * GELU_K * GELU_C) * u)
    act = act.astype(BF16)
    s.act[rows, :] = act
    s.blk[rows, :] = mid + nt(act, s.w2[...])
    cot = s.cot[rows, :]
    d_act = nn(cot.astype(BF16), s.w2[...])
    d_pre = (d_act * slope).astype(BF16)
    s.d_pre[rows, :] = d_pre
    d_hid2 = nt(d_pre, s.w1[...])
    s.gn[1:2, :] += jnp.sum(d_hid2 * normed2, axis=0, keepdims=True)
    s.d_mid[rows, :] = cot + norm_back(d_hid2 * s.n2[...], normed2, inv2)


def backward_window(wi, s):
    rows = pl.ds(pl.multiple_of(wi * WIN, WIN), WIN)
    z = wi // 4
    d_mid = s.d_mid[rows, :]
    d_att = nt(d_mid.astype(BF16), s.wp[...]).astype(BF16)
    dom = spread_heads(d_att)
    v = s.v[rows, :]
    p = s.p[wi]
    d_p = nt(dom, v)
    d_v = tn(p, dom).astype(BF16)
    pf = p.astype(F32)
    pd = pf * d_p
    d_s = pd - pf * jnp.sum(pd, axis=-1, keepdims=True)
    s.d_bias[0, pl.ds(z * 6, 6)] += d_s[:, :128].reshape(6, WIN, 128)
    s.d_bias[1, pl.ds(z * 6, 6), :, 0:16] += d_s[:, 128:].reshape(6, WIN, 16)
    d_low = d_s.astype(BF16)
    d_k = (tn(d_low, spread_heads(s.q[rows, :])) * LN2).astype(BF16)
    d_q = (pick_heads(nn(d_low, s.k[rows, :])) * SCALE).astype(BF16)
    s.dq[rows, :] = d_q
    s.dk[rows, :] = d_k
    s.dv[rows, :] = d_v
    d_win = nt(d_q, s.wq[0]) + nt(d_k, s.wq[1]) + nt(d_v, s.wq[2])
    d_hid = d_win.astype(BF16).astype(F32)
    normed1 = s.normed1[rows, :]
    s.gn[0:1, :] += jnp.sum(d_hid * normed1, axis=0, keepdims=True)
    s.x[rows, :] = d_mid + norm_back(d_hid * s.n1[...], normed1, s.inv1[rows, :])


def table_fold(d_bias_ref, can_ref, start, stop):
    lane = lax.broadcasted_iota(jnp.int32, (12, 256), 1)
    col = lane - (lane // 12) * 12

    def one(zh, carry):
        up = jnp.zeros((12, 256), F32)
        down = jnp.zeros((12, 256), F32)
        for c in range(12):
            x0 = d_bias_ref[0, zh, pl.ds(c, 12, stride=12), :]
            x1 = d_bias_ref[1, zh, pl.ds(c, 12, stride=12), :]
            x = jnp.concatenate([x0, x1], axis=1)
            over = jnp.where(col >= c, x, 0.0)
            up = up + (pltpu.roll(over, 256 - c, 1) if c else over)
            if c:
                down = down + pltpu.roll(x - over, 12 - c, 1)
        can_ref[zh, 0:12, :] = up
        can_ref[zh, 12:24, :] = down
        return carry

    lax.fori_loop(start, stop, one, 0)


def table_entries(idx_ref, sums, can_ref, lhs_ref, tab_ref, out_ref):
    can_ref[0:72, 0:128] = sums[0:72]
    for i in range(8):
        can_ref[9 * i : 9 * i + 9, 128:WIN] = sums[72:81, 16 * i : 16 * i + 16]
    entry = lax.broadcasted_iota(jnp.int32, (128, 256), 0)
    lane = lax.broadcasted_iota(jnp.int32, (1, 256), 1)
    spot = lane - (lane // 12) * 12
    acc = jnp.zeros((26 * 8, 128), F32)
    for part in range(2):
        for lr in range(12):
            idx = idx_ref[part * 16 + lr : part * 16 + lr + 1, :]
            ok = lane < WIN
            if part == 1:
                ok = ok & (spot > 0)
            hi = jnp.where(ok, idx >> 7, 99)
            here = jnp.where(entry == (idx & 127), 1.0, 0.0).astype(BF16)
            at = part * 12 + lr
            d = jnp.concatenate([can_ref[24 * k + at : 24 * k + at + 1, :] for k in range(3)] + [jnp.zeros((5, 256), F32)], axis=0)
            for a in range(26):
                lhs_ref[a * 8 : (a + 1) * 8, :] = jnp.where(hi == a, d, 0.0)
            acc = acc + nt(lhs_ref[...].astype(BF16), here)
    for a in range(26):
        tab_ref[3 * a : 3 * a + 3, :] = acc[8 * a : 8 * a + 3]
    out_ref[...] = tab_ref[0:80, :]


class Refs:
    pass


NAMES = [
    ("wq", (3, C, C), BF16),
    ("bias", (2, 12, WIN, 128), F32),
    ("d_bias", (2, 12, WIN, 128), F32),
    ("x", (TOK, C), F32),
    ("cot", (TOK, C), F32),
    ("blk", (TOK, C), F32),
    ("d_mid", (TOK, C), F32),
    ("normed1", (TOK, C), F32),
    ("inv1", (TOK, 1), F32),
    ("hid", (TOK, C), BF16),
    ("q", (TOK, C), BF16),
    ("k", (TOK, C), BF16),
    ("v", (TOK, C), BF16),
    ("p", (NWIN, 864, WIN), BF16),
    ("att", (TOK, C), BF16),
    ("hid2", (TOK, C), BF16),
    ("act", (TOK, FFN), BF16),
    ("d_pre", (TOK, FFN), BF16),
    ("dq", (TOK, C), BF16),
    ("dk", (TOK, C), BF16),
    ("dv", (TOK, C), BF16),
    ("gn", (8, C), F32),
    ("gall", (C, FFN), F32),
    ("can", (12, 24, 256), F32),
    ("pack", (96, 128), F32),
    ("rest", (72, 16), F32),
    ("idx", (32, 256), jnp.int32),
    ("own_can", (72, 256), F32),
    ("lhs", (26 * 8, 256), F32),
    ("tab", (80, 128), F32),
    ("slab", (2, 64, C), F32),
    ("ext_tok", (4, 6, 64, C), BF16),
    ("ext_cot", (4, 6, 64, C), BF16),
    ("e_blk", (4, 6, 64, C), BF16),
    ("e_tok", (4, 6, 64, C), BF16),
    ("f_own", (2 * C, FFN), BF16),
    ("f_sib", (2 * C, 384), BF16),
    ("f_core", (2 * C, 384), BF16),
    ("f_lon", (8, 48, 384), BF16),
    ("f_lat", (8, 48, 384), BF16),
    ("f_all", (8, 48, 384), BF16),
    ("t_own", (2, 8, 96, 128), BF16),
    ("t_sib", (8, 96, 128), BF16),
    ("t_core", (8, 96, 128), BF16),
    ("t_lon", (8, 96, 128), BF16),
    ("t_lat", (8, 96, 128), BF16),
    ("t_all", (8, 96, 128), BF16),
    ("zone_own", (8, 128), F32),
    ("zone_in", (8, 128), F32),
    ("table_in", (6, 1, POS), F32),
]


def pack_table(s):
    for p in range(12, 16):
        for k in range(3):
            zh = (p - 12) * 3 + k
            s.pack[24 * k : 24 * k + 24, :] = s.can[zh, :, 0:128]
            s.rest[24 * k : 24 * k + 24, :] = s.can[zh, :, 128:WIN]
        for i in range(8):
            s.pack[72:81, 16 * i : 16 * i + 16] = s.rest[9 * i : 9 * i + 9, :]
        s.t_own[p % 2, p // 2, 0:80, :] = s.pack[0:80, :].astype(BF16)
        if p == 12:
            for i in range(2):
                s.pack[88 + 2 * i : 89 + 2 * i, :] = s.gn[i : i + 1, 0:128]
                s.pack[89 + 2 * i : 90 + 2 * i, 0:64] = s.gn[i : i + 1, 128:C]
        else:
            s.pack[88:92, :] = jnp.zeros((4, 128), F32)
        s.t_own[p % 2, p // 2, 80:96, :] = s.pack[80:96, :].astype(BF16)


SEMS = [
    ("local", 16),
    ("in_send", 20),
    ("in_recv", 20),
    ("out_send", 18),
    ("out_recv", 18),
    ("core_send", 5),
    ("core_recv", 5),
] + [(name, 8) for name in ("fa_send", "fa_recv", "fb_send", "fb_recv", "fc_send", "fc_recv",
                            "ta_send", "ta_recv", "tb_send", "tb_recv", "tc_send", "tc_recv")]


def remote(src, dst, send, recv, where):
    return pltpu.make_async_remote_copy(
        src_ref=src, dst_ref=dst, send_sem=send, recv_sem=recv, device_id=where, device_id_type=pl.DeviceIdType.MESH
    )


def each_peer(count, me, start, stop, body):
    def one(p, carry):
        @pl.when(p != me)
        def _():
            body(p)

        return carry

    lax.fori_loop(start, stop, one, 0)


def main_kernel(
    tok, cot, n1, wqkv, wp, table, pos, mask, n2, w1, w2,
    blk_main, blk_cols, gtok_main, gtok_cols, f_res, t_res, *scratch
):
    s = Refs()
    for (name, _, _), ref in zip(NAMES, scratch):
        setattr(s, name, ref)
    for (name, _), ref in zip(SEMS, scratch[len(NAMES) :]):
        setattr(s, name, ref)
    s.n1, s.n2, s.wp, s.w1, s.w2 = n1, n2, wp, w1, w2
    lon = lax.axis_index("lon")
    lat = lax.axis_index("lat")
    lon_up, lon_down = lax.rem(lon + 1, 16), lax.rem(lon + 15, 16)
    lat_up, lat_down = lax.rem(lat + 1, 8), lax.rem(lat + 7, 8)
    chip = lon // 2
    core = lon - 2 * chip
    sibling = {"lon": lon + 1 - 2 * core, "lat": lat}
    barrier = pltpu.get_barrier_semaphore()

    def greet(a, b):
        pl.semaphore_signal(
            barrier, inc=1, device_id={"lon": a, "lat": b}, device_id_type=pl.DeviceIdType.MESH
        )

    for a in (lon_up, lon_down):
        for b in (lat_down, lat, lat_up):
            greet(a, b)
    each_peer(8, lat, 0, 8, lambda p: greet(lon, p))
    each_peer(8, chip, 0, 8, lambda p: greet(2 * p + core, lat))

    spans = ((1, 3), (3, 4), (0, 1))
    locals_in = []
    halo_in = [[], [], [], []]
    for i, (src, dst) in enumerate(((tok, s.ext_tok), (cot, s.ext_cot))):
        for n, (start, stop) in enumerate(spans):
            kept, gone, far = (slice(3, 6), slice(0, 3), lat_down) if n == 0 else (slice(0, 3), slice(3, 6), lat_up)
            a, b = src.at[start:stop], dst.at[start:stop]
            locals_in.append(pltpu.make_async_copy(a.at[:, kept], b.at[:, gone, 0:48], s.local.at[3 * i + n]))
            moves = (
                (a.at[:, gone], b.at[:, kept, 0:48], {"lon": lon, "lat": far}),
                (a.at[:, kept, 0:16], b.at[:, gone, 48:64], {"lon": lon_down, "lat": lat}),
                (a.at[:, gone, 0:16], b.at[:, kept, 48:64], {"lon": lon_down, "lat": far}),
            )
            for k, (a, b, where) in enumerate(moves):
                at = 9 * i + 3 * n + k
                copy = remote(a, b, s.in_send.at[at], s.in_recv.at[at], where)
                halo_in[2 * i + min(n, 1)].append(copy)
    for copy in locals_in:
        copy.start()
    zone_row(mask, s.zone_own)
    up = {"lon": lon, "lat": lat_up}
    table_copy = remote(table.at[6:12], s.table_in, s.in_send.at[18], s.in_recv.at[18], up)
    zone_copy = remote(s.zone_own, s.zone_in, s.in_send.at[19], s.in_recv.at[19], up)
    pl.semaphore_wait(barrier, 20)
    for copy in halo_in[0] + [zone_copy, table_copy] + halo_in[1]:
        copy.start()

    for i in range(3):
        s.wq[i] = wqkv[:, i * C : (i + 1) * C]
    for ref in (s.d_bias, s.gn, s.slab, s.pack, s.own_can, s.tab):
        ref[...] = jnp.zeros_like(ref)
    index_rows(pos, s.idx)
    prep_bias(0, table, s.idx, s.zone_own, s.bias)

    def arrived(group):
        for copy in halo_in[group]:
            copy.wait_recv()

    def window_loop(body, start, stop):
        lax.fori_loop(start, stop, lambda i, c: (body(i, s), c)[1], 0)

    def send_out(i, e, main, cols):
        copies = []
        for n, (start, stop) in enumerate(spans):
            kept, gone, far = (slice(3, 6), slice(0, 3), lat_up) if n == 0 else (slice(0, 3), slice(3, 6), lat_down)
            a, b, c = e.at[start:stop], main.at[start:stop], cols.at[start:stop]
            copy = pltpu.make_async_copy(a.at[:, gone, 0:48], b.at[:, kept], s.local.at[6 + 3 * i + n])
            copy.start()
            waits = [copy.wait]
            moves = (
                (a.at[:, kept, 0:48], b.at[:, gone], {"lon": lon, "lat": far}),
                (a.at[:, gone, 48:64], c.at[:, kept], {"lon": lon_up, "lat": lat}),
                (a.at[:, kept, 48:64], c.at[:, gone], {"lon": lon_up, "lat": far}),
            )
            for k, (a, b, where) in enumerate(moves):
                at = 9 * i + 3 * n + k
                copy = remote(a, b, s.out_send.at[at], s.out_recv.at[at], where)
                copy.start()
                waits += [copy.wait_send, copy.wait_recv]
            copies += waits
        return copies

    def chips_send(src_of, slots, send, recv, start, stop):
        def go(p):
            where = {"lon": 2 * p + core, "lat": lat}
            remote(src_of(p), slots.at[chip], send.at[p], recv.at[chip], where).start()

        each_peer(8, chip, start, stop, go)

    def chips_wait(src_of, slots, send, recv):
        def done(p):
            where = {"lon": 2 * p + core, "lat": lat}
            copy = remote(src_of(p), slots.at[p], send.at[p], recv.at[p], where)
            copy.wait_send()
            copy.wait_recv()

        each_peer(8, chip, 0, 8, done)

    def lat_send(slots, send, recv):
        def go(p):
            remote(slots.at[lat], slots.at[lat], send.at[p], recv.at[lat], {"lon": lon, "lat": p}).start()

        each_peer(8, lat, 0, 8, go)

    def lat_wait(slots, send, recv):
        def done(p):
            copy = remote(slots.at[lat], slots.at[p], send.at[p], recv.at[p], {"lon": lon, "lat": p})
            copy.wait_send()
            copy.wait_recv()

        each_peer(8, lat, 0, 8, done)

    def half(k):
        return pl.ds(pl.multiple_of(k * 384, 384), 384)

    def core_copy(i, src, dst):
        return remote(src, dst, s.core_send.at[i], s.core_recv.at[i], sibling)

    def f_piece(p):
        return s.f_core.at[pl.ds(pl.multiple_of(p * 48, 48), 48), :]

    def t_piece(p):
        return s.t_core.at[p]

    def f_done(p):
        return s.f_all.at[chip]

    def t_done(p):
        return s.t_all.at[chip]

    def total(slots, count):
        acc = slots[0].astype(F32)
        for i in range(1, count):
            acc = acc + slots[i].astype(F32)
        return acc

    def both(i, s):
        attention_window(i + 4, s)
        mlp_window(i, s)

    for copy in halo_in[2] + halo_in[3]:
        copy.start()
    locals_in[0].wait()
    arrived(0)
    assemble(s.ext_tok, s.x, 0)
    window_loop(attention_window, 0, 4)
    table_copy.wait()
    zone_copy.wait()
    prep_bias(1, s.table_in, s.idx, s.zone_in, s.bias)
    for copy in locals_in[1:3]:
        copy.wait()
    arrived(1)
    assemble(s.ext_tok, s.x, 1)
    locals_in[3].wait()
    arrived(2)
    assemble(s.ext_cot, s.cot, 0)
    window_loop(both, 0, 4)
    for copy in locals_in[4:6]:
        copy.wait()
    arrived(3)
    assemble(s.ext_cot, s.cot, 1)
    window_loop(mlp_window, 4, 8)
    for group in halo_in:
        for copy in group:
            copy.wait_send()
    s.f_own[0:C, :] = tn(s.hid2[...], s.d_pre[...]).astype(BF16)
    s.f_own[C : 2 * C, :] = tn(s.cot[...].astype(BF16), s.act[...]).astype(BF16)
    f_swap = core_copy(0, s.f_own.at[:, half(1 - core)], s.f_sib)
    f_swap.start()
    disassemble(s.blk, s.slab, s.e_blk)
    out_waits = send_out(0, s.e_blk, blk_main, blk_cols)
    f_swap.wait()
    s.f_core[...] = (s.f_own[:, half(core)].astype(F32) + s.f_sib[...].astype(F32)).astype(BF16)
    chips_send(f_piece, s.f_lon, s.fa_send, s.fa_recv, 0, 8)
    s.f_lon[chip] = f_piece(chip)[...]

    window_loop(backward_window, 0, 4)
    chips_wait(f_piece, s.f_lon, s.fa_send, s.fa_recv)
    s.f_lat[lat] = total(s.f_lon, 8).astype(BF16)
    lat_send(s.f_lat, s.fb_send, s.fb_recv)
    window_loop(backward_window, 4, 7)
    table_fold(s.d_bias, s.can, 0, 6)
    lat_wait(s.f_lat, s.fb_send, s.fb_recv)
    s.f_all[chip] = total(s.f_lat, 8).astype(BF16)
    chips_send(f_done, s.f_all, s.fc_send, s.fc_recv, 0, 8)
    window_loop(backward_window, 7, NWIN)

    hid = s.hid[...]
    s.gall[:, 0:C] = tn(hid, s.dq[...])
    s.gall[:, C : 2 * C] = tn(hid, s.dk[...])
    s.gall[:, 2 * C : 3 * C] = tn(hid, s.dv[...])
    s.gall[:, 3 * C : 4 * C] = tn(s.att[...], s.d_mid[...].astype(BF16))
    for p in range(12):
        for t in range(6):
            part = s.gall[p * 16 : (p + 1) * 16, t * 128 : (t + 1) * 128]
            s.t_own[p % 2, p // 2, t * 16 : (t + 1) * 16, :] = part.astype(BF16)
    t_swap = core_copy(1, s.t_own.at[1 - core, 0:6], s.t_sib.at[0:6])
    t_swap.start()
    table_fold(s.d_bias, s.can, 6, 12)
    pack_table(s)
    table_swap = core_copy(2, s.t_own.at[1 - core, 6:8], s.t_sib.at[6:8])
    table_swap.start()
    t_swap.wait()
    s.t_core[0:6] = (s.t_own[core, 0:6].astype(F32) + s.t_sib[0:6].astype(F32)).astype(BF16)
    chips_send(t_piece, s.t_lon, s.ta_send, s.ta_recv, 0, 6)
    table_swap.wait()
    s.t_core[6:8] = (s.t_own[core, 6:8].astype(F32) + s.t_sib[6:8].astype(F32)).astype(BF16)
    chips_send(t_piece, s.t_lon, s.ta_send, s.ta_recv, 6, 8)
    s.t_lon[chip] = s.t_core[chip]
    disassemble(s.x, s.slab, s.e_tok)
    out_waits += send_out(1, s.e_tok, gtok_main, gtok_cols)
    chips_wait(t_piece, s.t_lon, s.ta_send, s.ta_recv)
    s.t_lat[lat] = total(s.t_lon, 8).astype(BF16)
    lat_send(s.t_lat, s.tb_send, s.tb_recv)
    chips_wait(f_done, s.f_all, s.fc_send, s.fc_recv)
    f_back = core_copy(3, s.f_all, f_res.at[core])
    f_back.start()
    f_here = pltpu.make_async_copy(s.f_all, f_res.at[core], s.local.at[12])
    f_here.start()
    lat_wait(s.t_lat, s.tb_send, s.tb_recv)
    sums = total(s.t_lat, 8)

    @pl.when(chip < 6)
    def _():
        s.t_all[chip] = sums.astype(BF16)

    @pl.when(chip >= 6)
    def _():
        owner = jnp.where(chip == 7, lat_up, lat)
        table_entries(s.idx, s.t_lat[owner].astype(F32), s.own_can, s.lhs, s.tab, s.pack.at[0:80])
        s.t_all[chip, 0:80] = s.pack[0:80, :].astype(BF16)
        s.t_all[chip, 80:96] = sums[80:96].astype(BF16)

    chips_send(t_done, s.t_all, s.tc_send, s.tc_recv, 0, 8)
    f_back.wait()
    f_here.wait()
    for wait in out_waits:
        wait()
    chips_wait(t_done, s.t_all, s.tc_send, s.tc_recv)
    t_back = core_copy(4, s.t_all, t_res.at[core])
    t_back.start()
    t_here = pltpu.make_async_copy(s.t_all, t_res.at[core], s.local.at[13])
    t_here.start()
    t_back.wait()
    t_here.wait()


def finish_kernel(
    *refs
):
    far, outs, near, (w_full, sem) = refs[:6], refs[6:15], refs[15:21], refs[21:]
    block, gtok, gn1, gqkv, gproj, gtable, gn2, gfc1, gfc2 = outs
    blk_main, blk_cols, gtok_main, gtok_cols, f_res, t_res = near
    copies = [pltpu.make_async_copy(a, b, sem.at[i]) for i, (a, b) in enumerate(zip(far, near))]
    for copy in copies:
        copy.start()
    for copy in copies:
        copy.wait()
    col = lax.broadcasted_iota(jnp.int32, (16, C), 0)
    for main, cols, out in ((blk_main, blk_cols, block), (gtok_main, gtok_cols, gtok)):
        for level in range(4):
            for r in range(6):
                edge = jnp.where(col < 6, cols[level, r].astype(F32), main[level, r, 0:16, :].astype(F32))
                out[level, r, 0:16, :] = edge.astype(BF16)
                out[level, r, 16:48, :] = main[level, r, 16:48, :]
    for p in range(16):
        out = gfc1 if p < 8 else gfc2
        g, half = (p // 2) % 4, p % 2
        out[g * 48 : (g + 1) * 48, half * 384 : (half + 1) * 384] = f_res[p % 2, p // 2].astype(F32) * FACTOR
    for p in range(12):
        for t in range(6):
            part = t_res[p % 2, p // 2, t * 16 : (t + 1) * 16, :].astype(F32) * FACTOR
            w_full[p * 16 : (p + 1) * 16, t * 128 : (t + 1) * 128] = part
    gqkv[...] = w_full[:, 0:576]
    gproj[...] = w_full[:, 576:768]
    for p in range(12, 16):
        tab = t_res[p % 2, p // 2, 0:80, :].astype(F32) * FACTOR
        for a in range(26):
            width = min(128, POS - a * 128)
            for k in range(3):
                gtable[(p - 12) * 3 + k, :, a * 128 : a * 128 + width] = tab[a * 3 + k : a * 3 + k + 1, 0:width]
    norms = t_res[0, 6, 80:96, :].astype(F32) * FACTOR
    for i, out in enumerate((gn1, gn2)):
        out[:, 0:128] = norms[8 + 2 * i : 9 + 2 * i, :]
        out[:, 128:C] = norms[9 + 2 * i : 10 + 2 * i, 0:64]


def shards(tokens, norm1_gain, w_qkv, w_proj, bias_table, pos_index, mask_ids, norm2_gain, w_fc1, w_fc2, cotangent):
    vm = pl.BlockSpec(memory_space=pltpu.VMEM)
    anywhere = pl.BlockSpec(memory_space=pl.ANY)
    main = jax.ShapeDtypeStruct((4, 6, 48, C), BF16)
    cols = jax.ShapeDtypeStruct((4, 6, 16, C), BF16)
    outs = pl.pallas_call(
        main_kernel,
        out_shape=[
            main, cols, main, cols,
            jax.ShapeDtypeStruct((2, 8, 48, 384), BF16),
            jax.ShapeDtypeStruct((2, 8, 96, 128), BF16),
        ],
        in_specs=[anywhere] * 2 + [vm] * 5 + [pl.BlockSpec(memory_space=pltpu.SMEM)] + [vm] * 3,
        out_specs=[anywhere] * 6,
        scratch_shapes=[pltpu.VMEM(shape, dtype) for _, shape, dtype in NAMES]
        + [pltpu.SemaphoreType.DMA((n,)) for _, n in SEMS],
        compiler_params=pltpu.CompilerParams(
            vmem_limit_bytes=56 * 1024 * 1024, collective_id=0, has_side_effects=True
        ),
    )(
        tokens, cotangent, norm1_gain.reshape(1, C), w_qkv, w_proj,
        bias_table.transpose(0, 2, 1, 3).reshape(12, 1, POS), pos_index, mask_ids,
        norm2_gain.reshape(1, C), w_fc1, w_fc2.T,
    )
    f32 = lambda *shape: jax.ShapeDtypeStruct(shape, F32)
    block, gtok, gn1, gqkv, gproj, gtable, gn2, gfc1, gfc2 = pl.pallas_call(
        finish_kernel,
        out_shape=[main, main, f32(1, C), f32(C, 576), f32(C, C), f32(12, 1, POS), f32(1, C), f32(C, FFN), f32(C, FFN)],
        in_specs=[anywhere] * 6,
        out_specs=[vm] * 9,
        scratch_shapes=[pltpu.VMEM(out.shape, out.dtype) for out in outs]
        + [pltpu.VMEM((C, FFN), F32), pltpu.SemaphoreType.DMA((6,))],
        compiler_params=pltpu.CompilerParams(vmem_limit_bytes=56 * 1024 * 1024),
    )(*outs)
    gtable = gtable.reshape(2, 6, 1, POS).transpose(0, 2, 1, 3)
    return (block, gtok, gn1.reshape(C), gqkv, gproj, gtable, gn2.reshape(C), gfc1, gfc2.T)


def solution(mesh):
    act = P(None, "lat", "lon", None)
    table = P(None, "lat", None, None)
    return jax.shard_map(
        shards,
        mesh=mesh,
        in_specs=(act, P(), P(), P(), table, P(), P("lat"), P(), P(), P(), act),
        out_specs=(act, act, P(), P(), P(), table, P(), P(), P()),
        check_vma=False,
    )
```

time: 113 us -> 82.9 us (0.73)
  Pallas kernels: 102 us -> 82.1 us
  local copies, waits for them, and re-layouts: 9.24 us -> 0 us
    pallas_call x1, Pallas kernels: 101 us -> 78.6 us  [shards(): pl.pallas_call(main_kernel, out_shape=[main, cols, main, cols, jax.ShapeD...]
    unnamed x12 -> x0, local copies, waits for them, and re-layouts: 6.03 us -> none
    slice x4 -> x0, local copies, waits for them, and re-layouts: 2.28 us -> none  [the longest x2 1.27 us: index_tables(): down = pos_index[:, ::12].reshape(12, 12, 12)]
    pallas_call x1, Pallas kernels: 1.77 us -> 3.48 us  [shards(): pl.pallas_call(finish_kernel, out_shape=[main, main, f32(1, C), f32(C, 57...]
where the time goes in v2:
time: 82.9 us; the launch traced here: 82.7 us
  Pallas kernels  82.1 us (99%)
    pallas_call x1, Pallas kernels, shards(): pl.pallas_call(main_kernel, out_shape=[main, cols, main, cols, jax.ShapeD...  78.6 us
    pallas_call x1, Pallas kernels, shards(): pl.pallas_call(finish_kernel, out_shape=[main, main, f32(1, C), f32(C, 57...  3.48 us

profile of v2, /device:TPU:1, one launch (start us, length us, event | category | flops | bytes accessed | tf_op | source)
XLA Modules:
  0.0 82.7 jit_solution(7195809792468140498)
XLA Ops:
  0.6 78.6 %shard_map.178 = (bf16[4,6,48,192]{3,2,1,0:T(8,128)(2,1)}, bf16[4,6,16,192]{3,2,1,0:T(8,128)(2,1)}, bf16[4,6,48,192]{3,2,1,0:T(8,128)(2,1)}, bf16[4,6,16,192]{3,...) custom-call(bf16[4,6,48,192]{3,2,1,0:T(8,128)(2,1)} %tok.1, ...), custom_call_target="tpu_custom_call" | custom-call | tf_op jit(solution)/shard_map/pallas_call | solution.py:685
  79.2 3.5 %shard_map.179 = (bf16[4,6,48,192]{3,2,1,0:T(8,128)(2,1)}, bf16[4,6,48,192]{3,2,1,0:T(8,128)(2,1)}, f32[1,192]{1,0:T(1,128)}, f32[192,576]{1,0:T(8,128)}, f32[19...) custom-call(bf16[4,6,48,192]{3,2,1,0:T(8,128)(2,1)} %get-tuple-element, ...), custom_call_target="tpu_custom_call" | custom-call | tf_op jit(solution)/shard_map/pallas_call | solution.py:705

commit v3 on v2

--- a/solution.py
+++ b/solution.py
@@ -148,7 +148,7 @@
 
 
 def attention_window(wi, s):
-    rows = pl.ds(pl.multiple_of(wi * WIN, WIN), WIN)
+    rows = slice(wi * WIN, (wi + 1) * WIN)
     z = wi // 4
     x = s.x[rows, :]
     normed1, inv1 = norm_stats(x)
@@ -164,8 +164,8 @@
     qm = spread_heads(q)
     s.q[rows, :] = q
     scores = nt(qm, k)
-    b0 = s.bias[0, pl.ds(z * 6, 6)].reshape(864, 128)
-    b1 = s.bias[1, pl.ds(z * 6, 6)].reshape(864, 128)
+    b0 = s.bias[0, 6 * z : 6 * z + 6].reshape(864, 128)
+    b1 = s.bias[1, 6 * z : 6 * z + 6].reshape(864, 128)
     bias = jnp.concatenate([b0, b1], axis=1)[:, :WIN]
     e = jnp.exp2(scores + bias)
     p = (e * (1.0 / jnp.sum(e, axis=-1, keepdims=True))).astype(BF16)
@@ -176,7 +176,7 @@
 
 
 def mlp_window(wi, s):
-    rows = pl.ds(pl.multiple_of(wi * WIN, WIN), WIN)
+    rows = slice(wi * WIN, (wi + 1) * WIN)
     mid = s.blk[rows, :]
     normed2, inv2 = norm_stats(mid)
     hid2 = (normed2 * s.n2[...]).astype(BF16)
@@ -200,7 +200,7 @@
 
 
 def backward_window(wi, s):
-    rows = pl.ds(pl.multiple_of(wi * WIN, WIN), WIN)
+    rows = slice(wi * WIN, (wi + 1) * WIN)
     z = wi // 4
     d_mid = s.d_mid[rows, :]
     d_att = nt(d_mid.astype(BF16), s.wp[...]).astype(BF16)
@@ -212,8 +212,12 @@
     pf = p.astype(F32)
     pd = pf * d_p
     d_s = pd - pf * jnp.sum(pd, axis=-1, keepdims=True)
-    s.d_bias[0, pl.ds(z * 6, 6)] += d_s[:, :128].reshape(6, WIN, 128)
-    s.d_bias[1, pl.ds(z * 6, 6), :, 0:16] += d_s[:, 128:].reshape(6, WIN, 16)
+    d_s0, d_s1 = d_s[:, :128].reshape(6, WIN, 128), d_s[:, 128:].reshape(6, WIN, 16)
+    if wi % 4:
+        d_s0 = d_s0 + s.d_bias[0, 6 * z : 6 * z + 6]
+        d_s1 = d_s1 + s.d_bias[1, 6 * z : 6 * z + 6, :, 0:16]
+    s.d_bias[0, 6 * z : 6 * z + 6] = d_s0
+    s.d_bias[1, 6 * z : 6 * z + 6, :, 0:16] = d_s1
     d_low = d_s.astype(BF16)
     d_k = (tn(d_low, spread_heads(s.q[rows, :])) * LN2).astype(BF16)
     d_q = (pick_heads(nn(d_low, s.k[rows, :])) * SCALE).astype(BF16)
@@ -237,7 +241,7 @@
         for c in range(12):
             x0 = d_bias_ref[0, zh, pl.ds(c, 12, stride=12), :]
             x1 = d_bias_ref[1, zh, pl.ds(c, 12, stride=12), :]
-            x = jnp.concatenate([x0, x1], axis=1)
+            x = jnp.where(lane < WIN, jnp.concatenate([x0, x1], axis=1), 0.0)
             over = jnp.where(col >= c, x, 0.0)
             up = up + (pltpu.roll(over, 256 - c, 1) if c else over)
             if c:
@@ -281,6 +285,14 @@
 
 NAMES = [
     ("wq", (3, C, C), BF16),
+    ("n1", (1, C), F32),
+    ("wqkv", (C, 576), BF16),
+    ("wp", (C, C), BF16),
+    ("table", (12, 1, POS), F32),
+    ("pos", (WIN, WIN), jnp.int32),
+    ("n2", (1, C), F32),
+    ("w1", (C, FFN), BF16),
+    ("w2", (C, FFN), BF16),
     ("bias", (2, 12, WIN, 128), F32),
     ("d_bias", (2, 12, WIN, 128), F32),
     ("x", (TOK, C), F32),
@@ -318,8 +330,8 @@
     ("f_own", (2 * C, FFN), BF16),
     ("f_sib", (2 * C, 384), BF16),
     ("f_core", (2 * C, 384), BF16),
+    ("f_lat", (8, 48, 384), BF16),
     ("f_lon", (8, 48, 384), BF16),
-    ("f_lat", (8, 48, 384), BF16),
     ("f_all", (8, 48, 384), BF16),
     ("t_own", (2, 8, 96, 128), BF16),
     ("t_sib", (8, 96, 128), BF16),
@@ -352,7 +364,7 @@
 
 
 SEMS = [
-    ("local", 16),
+    ("local", 24),
     ("in_send", 20),
     ("in_recv", 20),
     ("out_send", 18),
@@ -389,7 +401,11 @@
         setattr(s, name, ref)
     for (name, _), ref in zip(SEMS, scratch[len(NAMES) :]):
         setattr(s, name, ref)
-    s.n1, s.n2, s.wp, s.w1, s.w2 = n1, n2, wp, w1, w2
+    fetched = {}
+    for i, (name, ref) in enumerate(
+        (("pos", pos), ("table", table), ("wqkv", wqkv), ("n1", n1), ("wp", wp), ("n2", n2), ("w1", w1), ("w2", w2))
+    ):
+        fetched[name] = pltpu.make_async_copy(ref, getattr(s, name), s.local.at[14 + i])
     lon = lax.axis_index("lon")
     lat = lax.axis_index("lat")
     lon_up, lon_down = lax.rem(lon + 1, 16), lax.rem(lon + 15, 16)
@@ -398,6 +414,8 @@
     core = lon - 2 * chip
     sibling = {"lon": lon + 1 - 2 * core, "lat": lat}
     barrier = pltpu.get_barrier_semaphore()
+    for name in ("pos", "table", "wqkv"):
+        fetched[name].start()
 
     def greet(a, b):
         pl.semaphore_signal(
@@ -437,19 +455,27 @@
     for copy in halo_in[0] + [zone_copy, table_copy] + halo_in[1]:
         copy.start()
 
+    for name in ("n1", "wp", "n2", "w1", "w2"):
+        fetched[name].start()
+    fetched["wqkv"].wait()
     for i in range(3):
-        s.wq[i] = wqkv[:, i * C : (i + 1) * C]
-    for ref in (s.d_bias, s.gn, s.slab, s.pack, s.own_can, s.tab):
+        s.wq[i] = s.wqkv[:, i * C : (i + 1) * C]
+    for ref in (s.gn, s.slab, s.pack, s.own_can, s.tab):
         ref[...] = jnp.zeros_like(ref)
-    index_rows(pos, s.idx)
-    prep_bias(0, table, s.idx, s.zone_own, s.bias)
+    fetched["pos"].wait()
+    index_rows(s.pos, s.idx)
+    fetched["table"].wait()
+    for name in ("n1", "wp", "n2", "w1", "w2"):
+        fetched[name].wait()
+    prep_bias(0, s.table, s.idx, s.zone_own, s.bias)
 
     def arrived(group):
         for copy in halo_in[group]:
             copy.wait_recv()
 
     def window_loop(body, start, stop):
-        lax.fori_loop(start, stop, lambda i, c: (body(i, s), c)[1], 0)
+        for i in range(start, stop):
+            body(i, s)
 
     def send_out(i, e, main, cols):
         copies = []
@@ -488,15 +514,15 @@
 
         each_peer(8, chip, 0, 8, done)
 
-    def lat_send(slots, send, recv):
+    def lat_send(src_of, slots, send, recv):
         def go(p):
-            remote(slots.at[lat], slots.at[lat], send.at[p], recv.at[lat], {"lon": lon, "lat": p}).start()
+            remote(src_of(p), slots.at[lat], send.at[p], recv.at[lat], {"lon": lon, "lat": p}).start()
 
         each_peer(8, lat, 0, 8, go)
 
-    def lat_wait(slots, send, recv):
+    def lat_wait(src_of, slots, send, recv):
         def done(p):
-            copy = remote(slots.at[lat], slots.at[p], send.at[p], recv.at[p], {"lon": lon, "lat": p})
+            copy = remote(src_of(p), slots.at[p], send.at[p], recv.at[p], {"lon": lon, "lat": p})
             copy.wait_send()
             copy.wait_recv()
 
@@ -515,7 +541,13 @@
         return s.t_core.at[p]
 
     def f_done(p):
-        return s.f_all.at[chip]
+        return s.f_all.at[lat]
+
+    def f_part(p):
+        return s.f_lon.at[chip]
+
+    def t_part(p):
+        return s.t_lat.at[lat]
 
     def t_done(p):
         return s.t_all.at[chip]
@@ -560,22 +592,21 @@
     f_swap = core_copy(0, s.f_own.at[:, half(1 - core)], s.f_sib)
     f_swap.start()
     disassemble(s.blk, s.slab, s.e_blk)
-    out_waits = send_out(0, s.e_blk, blk_main, blk_cols)
     f_swap.wait()
     s.f_core[...] = (s.f_own[:, half(core)].astype(F32) + s.f_sib[...].astype(F32)).astype(BF16)
-    chips_send(f_piece, s.f_lon, s.fa_send, s.fa_recv, 0, 8)
-    s.f_lon[chip] = f_piece(chip)[...]
+    lat_send(f_piece, s.f_lat, s.fa_send, s.fa_recv)
+    s.f_lat[lat] = f_piece(lat)[...]
 
     window_loop(backward_window, 0, 4)
-    chips_wait(f_piece, s.f_lon, s.fa_send, s.fa_recv)
-    s.f_lat[lat] = total(s.f_lon, 8).astype(BF16)
-    lat_send(s.f_lat, s.fb_send, s.fb_recv)
-    window_loop(backward_window, 4, 7)
+    lat_wait(f_piece, s.f_lat, s.fa_send, s.fa_recv)
+    s.f_lon[chip] = total(s.f_lat, 8).astype(BF16)
+    chips_send(f_part, s.f_lon, s.fb_send, s.fb_recv, 0, 8)
+    out_waits = send_out(0, s.e_blk, blk_main, blk_cols)
     table_fold(s.d_bias, s.can, 0, 6)
-    lat_wait(s.f_lat, s.fb_send, s.fb_recv)
-    s.f_all[chip] = total(s.f_lat, 8).astype(BF16)
-    chips_send(f_done, s.f_all, s.fc_send, s.fc_recv, 0, 8)
-    window_loop(backward_window, 7, NWIN)
+    window_loop(backward_window, 4, NWIN)
+    chips_wait(f_part, s.f_lon, s.fb_send, s.fb_recv)
+    s.f_all[lat] = total(s.f_lon, 8).astype(BF16)
+    lat_send(f_done, s.f_all, s.fc_send, s.fc_recv)
 
     hid = s.hid[...]
     s.gall[:, 0:C] = tn(hid, s.dq[...])
@@ -603,13 +634,13 @@
     out_waits += send_out(1, s.e_tok, gtok_main, gtok_cols)
     chips_wait(t_piece, s.t_lon, s.ta_send, s.ta_recv)
     s.t_lat[lat] = total(s.t_lon, 8).astype(BF16)
-    lat_send(s.t_lat, s.tb_send, s.tb_recv)
-    chips_wait(f_done, s.f_all, s.fc_send, s.fc_recv)
+    lat_send(t_part, s.t_lat, s.tb_send, s.tb_recv)
+    lat_wait(f_done, s.f_all, s.fc_send, s.fc_recv)
     f_back = core_copy(3, s.f_all, f_res.at[core])
     f_back.start()
     f_here = pltpu.make_async_copy(s.f_all, f_res.at[core], s.local.at[12])
     f_here.start()
-    lat_wait(s.t_lat, s.tb_send, s.tb_recv)
+    lat_wait(t_part, s.t_lat, s.tb_send, s.tb_recv)
     sums = total(s.t_lat, 8)
 
     @pl.when(chip < 6)
@@ -689,7 +720,7 @@
             jax.ShapeDtypeStruct((2, 8, 48, 384), BF16),
             jax.ShapeDtypeStruct((2, 8, 96, 128), BF16),
         ],
-        in_specs=[anywhere] * 2 + [vm] * 5 + [pl.BlockSpec(memory_space=pltpu.SMEM)] + [vm] * 3,
+        in_specs=[anywhere] * 7 + [pl.BlockSpec(memory_space=pltpu.SMEM)] + [anywhere] * 3,
         out_specs=[anywhere] * 6,
         scratch_shapes=[pltpu.VMEM(shape, dtype) for _, shape, dtype in NAMES]
         + [pltpu.SemaphoreType.DMA((n,)) for _, n in SEMS],

time: 82.9 us -> 77 us (0.929)
  Pallas kernels: 82.1 us -> 76 us
    pallas_call x1, Pallas kernels: 78.6 us -> 72.5 us  [shards(): pl.pallas_call(main_kernel, out_shape=[main, cols, main, cols, jax.ShapeD...]
where the time goes in v3:
time: 77 us; the launch traced here: 76.8 us
  Pallas kernels  76 us (99%)
  between operations  0.81 us (1%)
    pallas_call x1, Pallas kernels, shards(): pl.pallas_call(main_kernel, out_shape=[main, cols, main, cols, jax.ShapeD...  72.5 us
    pallas_call x1, Pallas kernels, shards(): pl.pallas_call(finish_kernel, out_shape=[main, main, f32(1, C), f32(C, 57...  3.48 us

profile of v3, /device:TPU:1, one launch (start us, length us, event | category | flops | bytes accessed | tf_op | source)
XLA Modules:
  0.0 76.8 jit_solution(7457242291838626824)
XLA Ops:
  0.6 72.5 %shard_map.178 = (bf16[4,6,48,192]{3,2,1,0:T(8,128)(2,1)}, bf16[4,6,16,192]{3,2,1,0:T(8,128)(2,1)}, bf16[4,6,48,192]{3,2,1,0:T(8,128)(2,1)}, bf16[4,6,16,192]{3,...) custom-call(bf16[4,6,48,192]{3,2,1,0:T(8,128)(2,1)} %tok.1, ...), custom_call_target="tpu_custom_call" | custom-call | tf_op jit(solution)/shard_map/pallas_call | solution.py:716
  73.2 3.5 %shard_map.179 = (bf16[4,6,48,192]{3,2,1,0:T(8,128)(2,1)}, bf16[4,6,48,192]{3,2,1,0:T(8,128)(2,1)}, f32[1,192]{1,0:T(1,128)}, f32[192,576]{1,0:T(8,128)}, f32[19...) custom-call(bf16[4,6,48,192]{3,2,1,0:T(8,128)(2,1)} %get-tuple-element, ...), custom_call_target="tpu_custom_call" | custom-call | tf_op jit(solution)/shard_map/pallas_call | solution.py:736

commit v4 on v3

--- a/solution.py
+++ b/solution.py
@@ -90,26 +90,35 @@
         zone_i = zone_i + jnp.where(row_i == r, here, 0.0)
         zone_j = zone_j + jnp.where(row_j == r, here, 0.0)
     mask = jnp.where(zone_i == zone_j, 0.0, -1e30)
-    idx = idx_ref[...]
+    groups = (
+        idx_ref[0:8, :],
+        idx_ref[16:24, :],
+        jnp.concatenate([idx_ref[8:12, :], idx_ref[24:28, :]], axis=0),
+    )
+    edge = lax.broadcasted_iota(jnp.int32, (8, 128), 1) < 16
+    rests = jnp.where(edge, groups[0][:, 128:], 0)
+    for g in (1, 2):
+        rests = rests + pltpu.roll(jnp.where(edge, groups[g][:, 128:], 0), 16 * g, 1)
+    idx = jnp.concatenate([x[:, :128] for x in groups] + [rests], axis=0)
     hi = idx >> 7
     lo = idx & 127
 
     def one(h, carry):
         row = table_ref[h] * LOG2E
-        tiles = []
-        for t in range(2):
-            lo_t = lo[:, t * 128 : (t + 1) * 128]
-            hi_t = hi[:, t * 128 : (t + 1) * 128]
-            acc = jnp.zeros((32, 128), F32)
-            for a in range(26):
-                part = row[:, a * 128 : min(POS, (a + 1) * 128)]
-                if a == 25:
-                    part = jnp.concatenate([part, jnp.zeros((1, 16), F32)], axis=1)
-                got = jnp.take_along_axis(jnp.broadcast_to(part, (32, 128)), lo_t, axis=1)
-                acc = jnp.where(hi_t == a, got, acc)
-            tiles.append(acc)
-        both = jnp.concatenate(tiles, axis=1)
-        upper, lower = both[:16], both[16:]
+        acc = jnp.zeros((32, 128), F32)
+        for a in range(26):
+            part = row[:, a * 128 : min(POS, (a + 1) * 128)]
+            if a == 25:
+                part = jnp.concatenate([part, jnp.zeros((1, 16), F32)], axis=1)
+            got = jnp.take_along_axis(jnp.broadcast_to(part, (32, 128)), lo, axis=1)
+            acc = jnp.where(hi == a, got, acc)
+        rest = acc[24:32]
+        wide = [
+            jnp.concatenate([acc[8 * g : 8 * g + 8], pltpu.roll(rest, 128 - 16 * g, 1) if g else rest], axis=1)
+            for g in range(3)
+        ]
+        upper = jnp.concatenate([wide[0], wide[2][0:4], wide[2][0:4]], axis=0)
+        lower = jnp.concatenate([wide[1], wide[2][4:8], wide[2][4:8]], axis=0)
         for c in range(12):
             ahead = pltpu.roll(upper, c, 1) if c else upper
             val = jnp.where(col >= c, ahead, pltpu.roll(lower, 256 - 12 + c, 1)) + mask
@@ -371,8 +380,8 @@
     ("out_recv", 18),
     ("core_send", 5),
     ("core_recv", 5),
-] + [(name, 8) for name in ("fa_send", "fa_recv", "fb_send", "fb_recv", "fc_send", "fc_recv",
-                            "ta_send", "ta_recv", "tb_send", "tb_recv", "tc_send", "tc_recv")]
+] + [(name, 8) for name in ("fa_send", "fa_recv", "fb_send", "fb_recv", "fc_send", "fc_recv")
+] + [(name, 16) for name in ("ta_send", "ta_recv", "tb_send", "tb_recv", "tc_send", "tc_recv")]
 
 
 def remote(src, dst, send, recv, where):
@@ -498,31 +507,44 @@
             copies += waits
         return copies
 
-    def chips_send(src_of, slots, send, recv, start, stop):
+    whole = (slice(None), 0)
+    parts = ((slice(0, 48), 0), (slice(48, 96), 8))
+
+    def chips_send(src_of, slots, send, recv, start, stop, part=whole):
+        rows, at = part
+
         def go(p):
             where = {"lon": 2 * p + core, "lat": lat}
-            remote(src_of(p), slots.at[chip], send.at[p], recv.at[chip], where).start()
+            remote(src_of(p).at[rows], slots.at[chip, rows], send.at[at + p], recv.at[at + chip], where).start()
 
         each_peer(8, chip, start, stop, go)
 
-    def chips_wait(src_of, slots, send, recv):
+    def chips_wait(src_of, slots, send, recv, part=whole):
+        rows, at = part
+
         def done(p):
             where = {"lon": 2 * p + core, "lat": lat}
-            copy = remote(src_of(p), slots.at[p], send.at[p], recv.at[p], where)
+            copy = remote(src_of(p).at[rows], slots.at[p, rows], send.at[at + p], recv.at[at + p], where)
             copy.wait_send()
             copy.wait_recv()
 
         each_peer(8, chip, 0, 8, done)
 
-    def lat_send(src_of, slots, send, recv):
+    def lat_send(src_of, slots, send, recv, part=whole):
+        rows, at = part
+
         def go(p):
-            remote(src_of(p), slots.at[lat], send.at[p], recv.at[lat], {"lon": lon, "lat": p}).start()
+            where = {"lon": lon, "lat": p}
+            remote(src_of(p).at[rows], slots.at[lat, rows], send.at[at + p], recv.at[at + lat], where).start()
 
         each_peer(8, lat, 0, 8, go)
 
-    def lat_wait(src_of, slots, send, recv):
+    def lat_wait(src_of, slots, send, recv, part=whole):
+        rows, at = part
+
         def done(p):
-            copy = remote(src_of(p), slots.at[p], send.at[p], recv.at[p], {"lon": lon, "lat": p})
+            where = {"lon": lon, "lat": p}
+            copy = remote(src_of(p).at[rows], slots.at[p, rows], send.at[at + p], recv.at[at + p], where)
             copy.wait_send()
             copy.wait_recv()
 
@@ -552,10 +574,10 @@
     def t_done(p):
         return s.t_all.at[chip]
 
-    def total(slots, count):
-        acc = slots[0].astype(F32)
+    def total(slots, count, rows=slice(None)):
+        acc = slots[0, rows].astype(F32)
         for i in range(1, count):
-            acc = acc + slots[i].astype(F32)
+            acc = acc + slots[i, rows].astype(F32)
         return acc
 
     def both(i, s):
@@ -625,41 +647,47 @@
     table_swap.start()
     t_swap.wait()
     s.t_core[0:6] = (s.t_own[core, 0:6].astype(F32) + s.t_sib[0:6].astype(F32)).astype(BF16)
-    chips_send(t_piece, s.t_lon, s.ta_send, s.ta_recv, 0, 6)
+    for part in parts:
+        chips_send(t_piece, s.t_lon, s.ta_send, s.ta_recv, 0, 6, part)
     table_swap.wait()
     s.t_core[6:8] = (s.t_own[core, 6:8].astype(F32) + s.t_sib[6:8].astype(F32)).astype(BF16)
-    chips_send(t_piece, s.t_lon, s.ta_send, s.ta_recv, 6, 8)
+    for part in parts:
+        chips_send(t_piece, s.t_lon, s.ta_send, s.ta_recv, 6, 8, part)
     s.t_lon[chip] = s.t_core[chip]
     disassemble(s.x, s.slab, s.e_tok)
     out_waits += send_out(1, s.e_tok, gtok_main, gtok_cols)
-    chips_wait(t_piece, s.t_lon, s.ta_send, s.ta_recv)
-    s.t_lat[lat] = total(s.t_lon, 8).astype(BF16)
-    lat_send(t_part, s.t_lat, s.tb_send, s.tb_recv)
+    for part in parts:
+        chips_wait(t_piece, s.t_lon, s.ta_send, s.ta_recv, part)
+        s.t_lat[lat, part[0]] = total(s.t_lon, 8, part[0]).astype(BF16)
+        lat_send(t_part, s.t_lat, s.tb_send, s.tb_recv, part)
     lat_wait(f_done, s.f_all, s.fc_send, s.fc_recv)
     f_back = core_copy(3, s.f_all, f_res.at[core])
     f_back.start()
     f_here = pltpu.make_async_copy(s.f_all, f_res.at[core], s.local.at[12])
     f_here.start()
-    lat_wait(t_part, s.t_lat, s.tb_send, s.tb_recv)
-    sums = total(s.t_lat, 8)
-
-    @pl.when(chip < 6)
-    def _():
-        s.t_all[chip] = sums.astype(BF16)
+    for part in parts:
+        lat_wait(t_part, s.t_lat, s.tb_send, s.tb_recv, part)
+
+        @pl.when(chip < 6)
+        def _():
+            s.t_all[chip, part[0]] = total(s.t_lat, 8, part[0]).astype(BF16)
+            chips_send(t_done, s.t_all, s.tc_send, s.tc_recv, 0, 8, part)
 
     @pl.when(chip >= 6)
     def _():
         owner = jnp.where(chip == 7, lat_up, lat)
         table_entries(s.idx, s.t_lat[owner].astype(F32), s.own_can, s.lhs, s.tab, s.pack.at[0:80])
         s.t_all[chip, 0:80] = s.pack[0:80, :].astype(BF16)
-        s.t_all[chip, 80:96] = sums[80:96].astype(BF16)
-
-    chips_send(t_done, s.t_all, s.tc_send, s.tc_recv, 0, 8)
+        s.t_all[chip, 80:96] = total(s.t_lat, 8, slice(80, 96)).astype(BF16)
+        for part in parts:
+            chips_send(t_done, s.t_all, s.tc_send, s.tc_recv, 0, 8, part)
+
     f_back.wait()
     f_here.wait()
     for wait in out_waits:
         wait()
-    chips_wait(t_done, s.t_all, s.tc_send, s.tc_recv)
+    for part in parts:
+        chips_wait(t_done, s.t_all, s.tc_send, s.tc_recv, part)
     t_back = core_copy(4, s.t_all, t_res.at[core])
     t_back.start()
     t_here = pltpu.make_async_copy(s.t_all, t_res.at[core], s.local.at[13])
@@ -677,15 +705,9 @@
     copies = [pltpu.make_async_copy(a, b, sem.at[i]) for i, (a, b) in enumerate(zip(far, near))]
     for copy in copies:
         copy.start()
-    for copy in copies:
-        copy.wait()
+    copies[4].wait()
+    copies[5].wait()
     col = lax.broadcasted_iota(jnp.int32, (16, C), 0)
-    for main, cols, out in ((blk_main, blk_cols, block), (gtok_main, gtok_cols, gtok)):
-        for level in range(4):
-            for r in range(6):
-                edge = jnp.where(col < 6, cols[level, r].astype(F32), main[level, r, 0:16, :].astype(F32))
-                out[level, r, 0:16, :] = edge.astype(BF16)
-                out[level, r, 16:48, :] = main[level, r, 16:48, :]
     for p in range(16):
         out = gfc1 if p < 8 else gfc2
         g, half = (p // 2) % 4, p % 2
@@ -706,6 +728,14 @@
     for i, out in enumerate((gn1, gn2)):
         out[:, 0:128] = norms[8 + 2 * i : 9 + 2 * i, :]
         out[:, 128:C] = norms[9 + 2 * i : 10 + 2 * i, 0:64]
+    for i in range(4):
+        copies[i].wait()
+    for main, cols, out in ((blk_main, blk_cols, block), (gtok_main, gtok_cols, gtok)):
+        for level in range(4):
+            for r in range(6):
+                edge = jnp.where(col < 6, cols[level, r].astype(F32), main[level, r, 0:16, :].astype(F32))
+                out[level, r, 0:16, :] = edge.astype(BF16)
+                out[level, r, 16:48, :] = main[level, r, 16:48, :]
 
 
 def shards(tokens, norm1_gain, w_qkv, w_proj, bias_table, pos_index, mask_ids, norm2_gain, w_fc1, w_fc2, cotangent):

time: 77 us -> 76.4 us (level)
    pallas_call x1, Pallas kernels: 72.5 us -> 71.7 us  [shards(): pl.pallas_call(main_kernel, out_shape=[main, cols, main, cols, jax.ShapeD...]
where the time goes in v4:
time: 76.4 us; the launch traced here: 76.2 us
  Pallas kernels  75.4 us (99%)
  between operations  0.81 us (1%)
    pallas_call x1, Pallas kernels, shards(): pl.pallas_call(main_kernel, out_shape=[main, cols, main, cols, jax.ShapeD...  71.7 us
    pallas_call x1, Pallas kernels, shards(): pl.pallas_call(finish_kernel, out_shape=[main, main, f32(1, C), f32(C, 57...  3.73 us

profile of v4, /device:TPU:1, one launch (start us, length us, event | category | flops | bytes accessed | tf_op | source)
XLA Modules:
  0.0 76.2 jit_solution(8821581250822173555)
XLA Ops:
  0.6 71.7 %shard_map.178 = (bf16[4,6,48,192]{3,2,1,0:T(8,128)(2,1)}, bf16[4,6,16,192]{3,2,1,0:T(8,128)(2,1)}, bf16[4,6,48,192]{3,2,1,0:T(8,128)(2,1)}, bf16[4,6,16,192]{3,...) custom-call(bf16[4,6,48,192]{3,2,1,0:T(8,128)(2,1)} %tok.1, ...), custom_call_target="tpu_custom_call" | custom-call | tf_op jit(solution)/shard_map/pallas_call | solution.py:746
  72.3 3.7 %shard_map.179 = (bf16[4,6,48,192]{3,2,1,0:T(8,128)(2,1)}, bf16[4,6,48,192]{3,2,1,0:T(8,128)(2,1)}, f32[1,192]{1,0:T(1,128)}, f32[192,576]{1,0:T(8,128)}, f32[19...) custom-call(bf16[4,6,48,192]{3,2,1,0:T(8,128)(2,1)} %get-tuple-element, ...), custom_call_target="tpu_custom_call" | custom-call | tf_op jit(solution)/shard_map/pallas_call | solution.py:766
